TPU v7x, 256 devices: a whole 4x4x8 slice. The times are simulated.
256 devices in a mesh: ctx: 32 (over y, z_lo, core), head: 8 (over x, z_hi).
Axes of the slice: x: 4, y: 4, z: 8 (z_hi: 2, z_lo: 4; z = z_hi * 4 + z_lo), core: 2. Of those that a mesh axis runs over, the one named last changes fastest.
Arguments:
- queries: bfloat16 [16384, 4096], P(('ctx', 'head')), may hold values from -3 to 3
- key_states: bfloat16 [16384, 1024], P(('ctx', 'head')), may hold values from -3 to 3
- value_states: bfloat16 [16384, 1024], P(('ctx', 'head')), may hold values from -4 to 4
- outputs: bfloat16 [16384, 4096], P(('ctx', 'head')), may hold values from -4 to 4
- out_grad: bfloat16 [16384, 4096], P(('ctx', 'head')), may hold values from -8 to 8
- log_sums: float32 [16384, 32], P('ctx', 'head'), may hold values from 6 to 9
- selected: int32 [32, 8, 8], P('ctx', 'head'), may hold values from -1 to 31, as said below
Outputs:
- query_grad: bfloat16 [16384, 4096], P(('ctx', 'head'))
- key_grad: bfloat16 [16384, 1024], P(('ctx', 'head'))
- value_grad: bfloat16 [16384, 1024], P(('ctx', 'head'))
Inputs may be any that keep to these rules, and one draw needn't show every extreme that they name: selected[c, g, 0] is c, the span's own block; the other entries of a list are distinct blocks earlier than c, chosen more often among early blocks, and -1 marks an empty entry; span c has min(8, c + 1) entries that are not -1.
All inputs are finite; a program needn't handle non-finite values.
Results may differ from a plain program's by a relative error of at most 0.0049.
Values may be sent and summed in bfloat16 or wider, within the bound.
No kernel may reach another device: no remote copies, remote signals or barrier semaphores. Data moves between devices by JAX's collectives and lax.ppermute only.
A program may use at most 192 MiB of HBM per device.

v0:
```python
import jax
import jax.numpy as jnp
from jax import lax
from jax.sharding import PartitionSpec as P

DH = 128
HQG = 4
BLOCK = 512
TOPK = 8


def for_sending(array):
    return jax.tree.map(lambda a: a.astype(jnp.bfloat16) if a.dtype == jnp.float32 else a, array)


def shards(queries, key_states, value_states, outputs, out_grad, log_sums, selected):
    query_heads, output_heads, grad_heads, key_heads, value_heads = (
        lax.all_to_all(queries, "head", split_axis=1, concat_axis=0, tiled=True),
        lax.all_to_all(outputs, "head", split_axis=1, concat_axis=0, tiled=True),
        lax.all_to_all(out_grad, "head", split_axis=1, concat_axis=0, tiled=True),
        lax.all_to_all(key_states, "head", split_axis=1, concat_axis=0, tiled=True),
        lax.all_to_all(value_states, "head", split_axis=1, concat_axis=0, tiled=True),
    )
    all_keys, all_values = (
        lax.all_gather(key_heads, "ctx", axis=0, tiled=True),
        lax.all_gather(value_heads, "ctx", axis=0, tiled=True),
    )
    local_tokens = query_heads.shape[0]
    spans = local_tokens // BLOCK
    groups = key_heads.shape[1] // DH
    pairs = spans * groups
    score_scale = DH ** (-0.5)
    first_span = lax.axis_index("ctx") * spans
    positions = jnp.arange(BLOCK, dtype=jnp.int32)

    def per_pair(flat_index):
        span_id = flat_index // groups
        group_id = flat_index % groups
        slot_ids = selected[span_id, group_id]
        live_slot = slot_ids >= 0
        safe_slot = jnp.where(live_slot, slot_ids, 0)
        keys_here = jnp.concatenate(
            [
                lax.dynamic_slice(
                    all_keys, (safe_slot[slot_number] * BLOCK, group_id * DH), (BLOCK, DH)
                )
                for slot_number in range(TOPK)
            ],
            axis=0,
        )
        values_here = jnp.concatenate(
            [
                lax.dynamic_slice(
                    all_values, (safe_slot[slot_number] * BLOCK, group_id * DH), (BLOCK, DH)
                )
                for slot_number in range(TOPK)
            ],
            axis=0,
        )
        key_pos = (safe_slot[:, None] * BLOCK + positions[None, :]).reshape(-1)
        key_live = jnp.repeat(live_slot, BLOCK)
        query_pos = (first_span + span_id) * BLOCK + positions
        allowed = key_live[None, :] & (key_pos[None, :] <= query_pos[:, None])
        query_parts = []
        key_sum = jnp.zeros((TOPK * BLOCK, DH), jnp.float32)
        value_sum = jnp.zeros((TOPK * BLOCK, DH), jnp.float32)
        for head_number in range(HQG):
            query_one = query_heads[:, head_number * DH : (head_number + 1) * DH]
            output_one = output_heads[:, head_number * DH : (head_number + 1) * DH]
            grad_one = grad_heads[:, head_number * DH : (head_number + 1) * DH]
            scores = (
                jnp.einsum("qd,kd->qk", query_one, keys_here, preferred_element_type=jnp.float32)
                * score_scale
            )
            weights = jnp.where(allowed, jnp.exp(scores - log_sums[:, head_number][:, None]), 0.0)
            probs_low = weights.astype(jnp.bfloat16)
            grad_probs = jnp.einsum(
                "qd,kd->qk", grad_one, values_here, preferred_element_type=jnp.float32
            )
            row_delta = jnp.sum(
                grad_one.astype(jnp.float32) * output_one.astype(jnp.float32), axis=1
            )
            grad_low = (weights * (grad_probs - row_delta[:, None])).astype(jnp.bfloat16)
            query_parts.append(
                (
                    jnp.dot(grad_low, keys_here, preferred_element_type=jnp.float32) * score_scale
                ).astype(jnp.bfloat16)
            )
            key_sum = (
                key_sum
                + jnp.einsum("qk,qd->kd", grad_low, query_one, preferred_element_type=jnp.float32)
                * score_scale
            )
            value_sum = value_sum + jnp.einsum(
                "qk,qd->kd", probs_low, grad_one, preferred_element_type=jnp.float32
            )
        query_out = jnp.concatenate(query_parts, axis=1)
        return (query_out, key_sum, value_sum)

    query_stack, first_store, second_store = lax.map(per_pair, jnp.arange(pairs, dtype=jnp.int32))
    query_local = (
        query_stack.reshape(spans, groups, BLOCK, HQG * DH)
        .transpose(0, 2, 1, 3)
        .reshape(local_tokens, groups * HQG * DH)
    )
    key_width = groups * DH

    def place(flat_index, dense_sums):
        key_dense, value_dense = dense_sums
        pair_index = flat_index // TOPK
        slot_number = flat_index % TOPK
        span_id = pair_index // groups
        group_id = pair_index % groups
        slot_block = selected[span_id, group_id, slot_number]
        block_id = jnp.maximum(slot_block, 0)
        live_factor = jnp.where(slot_block >= 0, 1.0, 0.0).astype(jnp.float32)
        corner = (block_id * BLOCK, group_id * DH)
        key_piece = (
            lax.dynamic_slice(first_store, (pair_index, slot_number * BLOCK, 0), (1, BLOCK, DH))[0]
            * live_factor
        )
        value_piece = (
            lax.dynamic_slice(second_store, (pair_index, slot_number * BLOCK, 0), (1, BLOCK, DH))[0]
            * live_factor
        )
        key_dense = lax.dynamic_update_slice(
            key_dense, lax.dynamic_slice(key_dense, corner, (BLOCK, DH)) + key_piece, corner
        )
        value_dense = lax.dynamic_update_slice(
            value_dense, lax.dynamic_slice(value_dense, corner, (BLOCK, DH)) + value_piece, corner
        )
        return (key_dense, value_dense)

    sequence_rows = all_keys.shape[0]
    empty_sums = jnp.zeros((sequence_rows, key_width), jnp.float32)
    key_dense, value_dense = lax.fori_loop(0, pairs * TOPK, place, (empty_sums, empty_sums))
    key_own, value_own = (
        lax.psum_scatter(key_dense, "ctx", scatter_dimension=0, tiled=True),
        lax.psum_scatter(value_dense, "ctx", scatter_dimension=0, tiled=True),
    )
    query_grad, key_grad, value_grad = (
        lax.all_to_all(
            for_sending(query_local), "head", split_axis=0, concat_axis=1, tiled=True
        ).astype(query_local.dtype),
        lax.all_to_all(
            key_own.astype(jnp.bfloat16), "head", split_axis=0, concat_axis=1, tiled=True
        ),
        lax.all_to_all(
            value_own.astype(jnp.bfloat16), "head", split_axis=0, concat_axis=1, tiled=True
        ),
    )
    return (query_grad, key_grad, value_grad)


def solution(mesh):
    return jax.shard_map(
        shards,
        mesh=mesh,
        in_specs=(
            P(("ctx", "head"), None),
            P(("ctx", "head"), None),
            P(("ctx", "head"), None),
            P(("ctx", "head"), None),
            P(("ctx", "head"), None),
            P("ctx", "head"),
            P("ctx", "head", None),
        ),
        out_specs=(P(("ctx", "head"), None), P(("ctx", "head"), None), P(("ctx", "head"), None)),
        check_vma=False,
    )
```

profile of v0, /device:TPU:2, one launch (start us, length us, event | category | flops | bytes accessed | tf_op | source)
XLA Modules:
  0.0 637.0 jit_solution(12641626702631867127)
XLA Ops:
  8.1 20.3 %all_to_all.152 = bf16[64,8,128]{2,0,1:T(8,128)(2,1)} all-to-all(bf16[64,8,128]{2,0,1:T(8,128)(2,1)S(1)} %copy_bitcast_fusion.6), channel_id=1, replica_groups=mesh['ctx'=32,'head'=8] {'head'}, dimensions={1} | all-to-all | bytes 262144 | tf_op jit(solution)/shard_map/all_to_all | solution.py:21
  29.4 13.7 %all_to_all.153 = bf16[64,8,128]{2,0,1:T(8,128)(2,1)} all-to-all(bf16[64,8,128]{2,0,1:T(8,128)(2,1)S(1)} %copy_bitcast_fusion.5), channel_id=1, replica_groups=mesh['ctx'=32,'head'=8] {'head'}, dimensions={1} | all-to-all | bytes 262144 | tf_op jit(solution)/shard_map/all_to_all | solution.py:22
  45.0 5.0 all-to-all-start.4
  58.2 12.2 %all-to-all-done.4 = bf16[64,8,512]{2,0,1:T(8,128)(2,1)S(1)} async-done(((bf16[64,8,512]{2,0,1:T(8,128)(2,1)}), bf16[64,8,512]{2,0,1:T(8,128)(2,1)S(1)}, u32[]{:S(2)}, u32[]{:S(2)}) %all-to-all-start.4) | async-done | bytes 524320 | tf_op jit(solution)/shard_map/all_to_all | solution.py:19
  70.4 6.5 %all-to-all-start.3 = ((bf16[64,8,512]{2,0,1:T(8,128)(2,1)}), bf16[64,8,512]{2,0,1:T(8,128)(2,1)S(1)}, u32[]{:S(2)}, u32[]{:S(2)}) async-start(bf16[64,8,512]{2,0,1:T(8,128)(2,1)} %bitcast.136), calls=%async_computation.3 | async-start | bytes 1048576 | tf_op jit(solution)/shard_map/all_to_all | solution.py:20
  77.9 13.8 %all-to-all-done.3 = bf16[64,8,512]{2,0,1:T(8,128)(2,1)S(1)} async-done(((bf16[64,8,512]{2,0,1:T(8,128)(2,1)}), bf16[64,8,512]{2,0,1:T(8,128)(2,1)S(1)}, u32[]{:S(2)}, u32[]{:S(2)}) %all-to-all-start.3) | async-done | bytes 524320 | tf_op jit(solution)/shard_map/all_to_all | solution.py:20
  91.7 6.3 all-to-all-start.1
  98.3 3.4 all-gather.3.cloned.1.call-done
  101.8 78.1 %all-gather.5.cloned.1.call-done = bf16[16384,128]{1,0:T(8,128)(2,1)} async-done(((bf16[512,128]{1,0:T(8,128)(2,1)}), bf16[16384,128]{1,0:T(8,128)(2,1)}) %all-gather.5.cloned.1.call-update) | async-done | bytes 4194320 | tf_op jit(solution)/shard_map/all_gather | solution.py:26
  188.1 2.8 bitcast_select_fusion
  193.7 4.6 bitcast_select_fusion.2
  198.4 3.7 bitcast_select_fusion.3
  217.0 4.5 fusion.4
  230.9 2.9 fusion.5
  242.7 3.5 broadcast_in_dim.46.clone
  246.2 3.6 broadcast_in_dim.46
  249.8 30.7 %while.11 = (s32[]{:T(128)}, f32[16384,128]{1,0:T(8,128)}, f32[16384,128]{1,0:T(8,128)}, s32[1,1,8]{2,1,0:T(1,128)S(1)}, f32[1,4096,128]{2,1,0:T(8,128)}, /*inde...) while((s32[]{:T(128)}, f32[16384,128]{1,0:T(8,128)}, ...), condition=%wide.region_5.6_spmd, body=%wide.region_4.5_spmd.sunk | while | flops 262166 | bytes 1573763 | solution.py:136
  281.8 3.1 fusion.17
  291.5 8.6 %all-to-all-start.5 = ((bf16[8,64,512]{2,1,0:T(8,128)(2,1)}), bf16[8,64,512]{2,1,0:T(8,128)(2,1)S(1)}, u32[]{:S(2)}, u32[]{:S(2)}) async-start(bf16[8,64,512]{2,1,0:T(8,128)(2,1)} %bitcast.38), calls=%async_computation.5 | async-start | bytes 1048576 | tf_op jit(solution)/shard_map/all_to_all | solution.py:142
  300.1 147.6 %reduce-scatter.3.cloned.1.call-done = f32[512,128]{1,0:T(8,128)} async-done(((f32[16384,128]{1,0:T(8,128)}), f32[512,128]{1,0:T(8,128)}) %reduce-scatter.3.cloned.1.call-update) | async-done | bytes 262160 | tf_op jit(solution)/shard_map/reduce_scatter | solution.py:138
  449.3 9.3 %all-to-all-start.6 = ((bf16[8,64,128]{2,1,0:T(8,128)(2,1)}), bf16[8,64,128]{2,1,0:T(8,128)(2,1)S(1)}, u32[]{:S(2)}, u32[]{:S(2)}) async-start(bf16[8,64,128]{2,1,0:T(8,128)(2,1)} %bitcast.42), calls=%async_computation.7 | async-start | bytes 262144 | tf_op jit(solution)/shard_map/all_to_all | solution.py:145
  459.5 151.5 %reduce-scatter.5.cloned.1.call-done = f32[512,128]{1,0:T(8,128)} async-done(((f32[16384,128]{1,0:T(8,128)}), f32[512,128]{1,0:T(8,128)}) %reduce-scatter.5.cloned.1.call-update) | async-done | bytes 262160 | tf_op jit(solution)/shard_map/reduce_scatter | solution.py:139
  612.6 8.2 %all-to-all-start.7 = ((bf16[8,64,128]{2,1,0:T(8,128)(2,1)}), bf16[8,64,128]{2,1,0:T(8,128)(2,1)S(1)}, u32[]{:S(2)}, u32[]{:S(2)}) async-start(bf16[8,64,128]{2,1,0:T(8,128)(2,1)} %bitcast.44), calls=%async_computation.9 | async-start | bytes 262144 | tf_op jit(solution)/shard_map/all_to_all | solution.py:148
  621.5 8.3 %all-to-all-done.7 = bf16[8,64,128]{2,1,0:T(8,128)(2,1)S(1)} async-done(((bf16[8,64,128]{2,1,0:T(8,128)(2,1)}), bf16[8,64,128]{2,1,0:T(8,128)(2,1)S(1)}, u32[]{:S(2)}, u32[]{:S(2)}) %all-to-all-start.7) | async-done | bytes 131104 | tf_op jit(solution)/shard_map/all_to_all | solution.py:148
  (122 shorter events, 85.8 us)
Async XLA Ops:
  7.2 69.7 %copy-start.20 = (s32[1,1,8]{2,1,0:T(1,128)S(1)}, s32[1,1,8]{2,1,0:T(1,128)}, u32[]{:S(2)}) copy-start(s32[1,1,8]{2,1,0:T(1,128)} %param.15) | copy-start | bytes 100
  7.2 69.8 %copy-start.16 = (bf16[64,4096]{1,0:T(8,128)(2,1)S(1)}, bf16[64,4096]{1,0:T(8,128)(2,1)}, u32[]{:S(2)}) copy-start(bf16[64,4096]{1,0:T(8,128)(2,1)} %param.9) | copy-start | bytes 1572868
  7.2 70.7 %copy-start.21 = (f32[512,4]{0,1:T(4,128)S(1)}, f32[512,4]{0,1:T(4,128)}, u32[]{:S(2)}) copy-start(f32[512,4]{0,1:T(4,128)} %param.14) | copy-start | bytes 24580
  7.2 94.6 %all-gather.3.cloned.1.call-start = ((), (), s32[]{:S(2)}) async-start(), calls=%async_computation.10 | async-start | bytes 4325376 | tf_op jit(solution)/shard_map/all_gather | solution.py:25
  28.5 151.5 %all-gather.5.cloned.1.call-start = ((), (), s32[]{:S(2)}) async-start(), calls=%async_computation.11 | async-start | bytes 4325376 | tf_op jit(solution)/shard_map/all_gather | solution.py:26
  45.0 25.3 %all-to-all-start.4 = ((bf16[64,8,512]{2,0,1:T(8,128)(2,1)}), bf16[64,8,512]{2,0,1:T(8,128)(2,1)S(1)}, u32[]{:S(2)}, u32[]{:S(2)}) async-start(bf16[64,8,512]{2,0,1:T(8,128)(2,1)} %bitcast.135), calls=%async_computation.4 | async-start | bytes 1048576 | tf_op jit(solution)/shard_map/all_to_all | solution.py:19
  70.4 21.4 %all-to-all-start.3 = ((bf16[64,8,512]{2,0,1:T(8,128)(2,1)}), bf16[64,8,512]{2,0,1:T(8,128)(2,1)S(1)}, u32[]{:S(2)}, u32[]{:S(2)}) async-start(bf16[64,8,512]{2,0,1:T(8,128)(2,1)} %bitcast.136), calls=%async_computation.3 | async-start | bytes 1048576 | tf_op jit(solution)/shard_map/all_to_all | solution.py:20
  91.7 99.2 %copy-start.9 = (bf16[64,8,512]{2,0,1:T(8,128)(2,1)}, bf16[64,8,512]{2,0,1:T(8,128)(2,1)S(1)}, u32[]{:S(2)}) copy-start(bf16[64,8,512]{2,0,1:T(8,128)(2,1)S(1)} %all-to-all-done.3) | copy-start | bytes 1572868
  91.7 96.4 %all-to-all-start.1 = ((bf16[64,8,512]{2,0,1:T(8,128)(2,1)}), bf16[64,8,512]{2,0,1:T(8,128)(2,1)S(1)}, u32[]{:S(2)}, u32[]{:S(2)}) async-start(bf16[64,8,512]{2,0,1:T(8,128)(2,1)} %bitcast.137), calls=%async_computation.1 | async-start | bytes 1048576 | tf_op jit(solution)/shard_map/all_to_all | solution.py:18
  98.0 349.7 %reduce-scatter.3.cloned.1.call-start = ((), (), s32[]{:S(2)}) async-start(), calls=%async_computation.12 | async-start | bytes 8650752 | tf_op jit(solution)/shard_map/reduce_scatter | solution.py:138
  188.1 2.9 copy-start.17
  193.7 4.7 copy-start.18
  198.4 3.7 copy-start.10
  224.3 14.6 %copy-start.4 = (bf16[512,4096]{0,1:T(8,128)(2,1)}, bf16[512,4096]{0,1:T(8,128)(2,1)S(1)}, u32[]{:S(2)}) copy-start(bf16[512,4096]{0,1:T(8,128)(2,1)S(1)} %fusion.3) | copy-start | bytes 12582916
  229.6 10.5 %copy-start.6 = (bf16[512,4096]{0,1:T(8,128)(2,1)}, bf16[512,4096]{0,1:T(8,128)(2,1)S(1)}, u32[]{:S(2)}) copy-start(bf16[512,4096]{0,1:T(8,128)(2,1)S(1)} %fusion.2) | copy-start | bytes 12582916
  230.9 3.0 copy-start.15
  233.9 5.0 copy-start.7
  233.9 3.7 copy-start.2
  280.6 330.4 %reduce-scatter.5.cloned.1.call-start = ((), (), s32[]{:S(2)}) async-start(), calls=%async_computation.13 | async-start | bytes 8650752 | tf_op jit(solution)/shard_map/reduce_scatter | solution.py:139
  281.8 3.4 copy-start.5
  289.7 340.8 %copy-start.1 = (bf16[64,1024]{1,0:T(8,128)(2,1)S(1)}, bf16[64,1024]{1,0:T(8,128)(2,1)}, u32[]{:S(2)}) copy-start(bf16[64,1024]{1,0:T(8,128)(2,1)} %param.10) | copy-start | bytes 393220
  291.5 157.8 %all-to-all-start.5 = ((bf16[8,64,512]{2,1,0:T(8,128)(2,1)}), bf16[8,64,512]{2,1,0:T(8,128)(2,1)S(1)}, u32[]{:S(2)}, u32[]{:S(2)}) async-start(bf16[8,64,512]{2,1,0:T(8,128)(2,1)} %bitcast.38), calls=%async_computation.5 | async-start | bytes 1048576 | tf_op jit(solution)/shard_map/all_to_all | solution.py:142
  449.3 163.3 %all-to-all-start.6 = ((bf16[8,64,128]{2,1,0:T(8,128)(2,1)}), bf16[8,64,128]{2,1,0:T(8,128)(2,1)S(1)}, u32[]{:S(2)}, u32[]{:S(2)}) async-start(bf16[8,64,128]{2,1,0:T(8,128)(2,1)} %bitcast.42), calls=%async_computation.7 | async-start | bytes 262144 | tf_op jit(solution)/shard_map/all_to_all | solution.py:145
  612.6 17.2 %all-to-all-start.7 = ((bf16[8,64,128]{2,1,0:T(8,128)(2,1)}), bf16[8,64,128]{2,1,0:T(8,128)(2,1)S(1)}, u32[]{:S(2)}, u32[]{:S(2)}) async-start(bf16[8,64,128]{2,1,0:T(8,128)(2,1)} %bitcast.44), calls=%async_computation.9 | async-start | bytes 262144 | tf_op jit(solution)/shard_map/all_to_all | solution.py:148
  (8 other events, 17.5 us)
Sparse Core Ops, SparseCore 0:
  28.6 73.1 all-gather.2
  103.6 76.2 all-gather.4
  280.7 166.9 reduce-scatter.2
  450.1 160.8 reduce-scatter.4
where the time goes:
time: 639 us; the launch traced here: 637 us
  waiting for transfers between devices  416 us (65%)
  matrix products  46.6 us (7%)
  starting transfers between devices  44 us (7%)
  local copies, waits for them, and re-layouts  42.8 us (7%)
  blocking collectives  34 us (5%)
  other arithmetic  24.6 us (4%)
  between operations  19 us (3%)
  loops' own time  10.5 us (2%)
    reduce_scatter x1, waiting for transfers between devices, shards(): lax.psum_scatter(value_dense, 'ctx', scatter_dimension=0, tiled=True)  151 us
    reduce_scatter x1, waiting for transfers between devices, shards(): lax.psum_scatter(key_dense, 'ctx', scatter_dimension=0, tiled=True)  148 us
    all_gather x1, waiting for transfers between devices, shards(): lax.all_gather(value_heads, 'ctx', axis=0, tiled=True)  78.1 us
    unnamed x60, local copies, waits for them, and re-layouts  23.7 us
    all_to_all x1, blocking collectives, shards(): lax.all_to_all(key_states, 'head', split_axis=1, concat_axis=0, tiled=True)  20.3 us
    dynamic_update_slice x8, other arithmetic, place(): lax.dynamic_update_slice(value_dense, lax.dynamic_slice(value_dense, corn...  15.6 us
    dot_general x4, matrix products, per_pair(): jnp.einsum('qd,kd->qk', query_one, keys_here, preferred_element_type=jnp....  13.9 us
    all_to_all x1, waiting for transfers between devices, shards(): lax.all_to_all(out_grad, 'head', split_axis=1, concat_axis=0, tiled=True)  13.8 us
  transfers between devices with their start and end apart: 10, of which 7 were waited for; matrix products, arithmetic and copies ran while one was open for 4% of the time, Pallas kernels for 0%

commit v1 on v0

v1 whole, which is shorter than its diff:
```python
import functools

import jax
import jax.numpy as jnp
from jax import lax
from jax.experimental import pallas as pl
from jax.experimental.pallas import tpu as pltpu
from jax.sharding import Mesh, PartitionSpec as P

DH = 128
HQG = 4
BLOCK = 512
TOPK = 8
GROUPS = 8
NB = 32
SHARD = 64
CHUNK = 128
ROWS = 512
KEYS = 512
SCALE = DH ** (-0.5)
LOG2E = 1.4426950408889634
ZH = ("z", "h")
ZCH = ("z", "c", "h")
PLANE = ("y", "c", "x")
OFFSETS = (0, 1, -1, 2)
BF = jnp.bfloat16
F32 = jnp.float32


def plane_index(y, c, x):
    return ((y % 4) * 2 + c) * 4 + (x % 4)


def shift(array, phase, distance):
    pairs = []
    for y in range(4):
        for c in range(2):
            for x in range(4):
                along_x = (c == 0) == (phase == 0)
                target = plane_index(y, c, x + distance) if along_x else plane_index(y + distance, c, x)
                pairs.append((plane_index(y, c, x), target))
    return lax.ppermute(array, PLANE, pairs)


def swap(array):
    return lax.ppermute(array, "c", [(0, 1), (1, 0)])


def spread(own):
    first = [own] + [shift(own, 0, -d) for d in OFFSETS[1:]]
    row = jnp.concatenate(first, axis=0)
    mine = [row] + [shift(row, 1, -d) for d in OFFSETS[1:]]
    return mine, [swap(m) for m in mine]


def total(*terms):
    return functools.reduce(lambda a, b: a + b, [t.astype(F32) for t in terms])


def ring_sum(own, plus, minus, far, phase):
    half = far.shape[0] // 2
    low = shift(far[:half], phase, 1)
    high = shift(far[half:], phase, -1)
    plus = jnp.concatenate(
        [total(*[p[:half] for p in plus], low), total(*[p[half:] for p in plus])], axis=0
    )
    minus = jnp.concatenate(
        [total(*[m[:half] for m in minus]), total(*[m[half:] for m in minus], high)], axis=0
    )
    got_plus = shift(plus.astype(BF), phase, 1)
    got_minus = shift(minus.astype(BF), phase, -1)
    return total(*own, got_plus, got_minus)


def gather_sums(theirs_far, theirs_near, mine_far, mine_near):
    far = total(mine_far, swap(theirs_far)).astype(BF)
    size = far.shape[0]
    near = [mine_near, swap(theirs_near)]
    cut = lambda i: [a[i * size : (i + 1) * size] for a in near]
    part = ring_sum(cut(0), cut(1), cut(2), far, 0)
    size //= 4
    cut = lambda i: part[i * size : (i + 1) * size]
    return ring_sum([cut(0)], [cut(1)], [cut(2)], cut(3).astype(BF), 1).astype(BF)


def kernel(
    meta, chosen, lse_ref, delta_ref, qdo_ref,
    w0, w1, w2, w3, o0, o1, o2, o3,
    theirs_far, theirs_near, mine_far, mine_near, dq_ref,
    kv, acc, q_t, do_t, dq_t, sems,
):
    x, y, core = meta[0], meta[1], meta[2]

    def place(owner_core, d1, d2):
        on_x = owner_core == 0
        return (
            lax.rem(x + jnp.where(on_x, d1, d2) + 4, 4),
            lax.rem(y + jnp.where(on_x, d2, d1) + 4, 4),
        )

    copies = []
    for which, refs in ((core, (w0, w1, w2, w3)), (1 - core, (o0, o1, o2, o3))):
        for i2, ref in enumerate(refs):
            for i1 in range(4):
                xb, yb = place(which, OFFSETS[i1], OFFSETS[i2])
                copy = pltpu.make_async_copy(
                    ref.at[pl.ds(i1 * 8, 8)],
                    kv.at[which, pl.ds(yb * 8, 8), pl.ds(pl.multiple_of(xb * CHUNK, CHUNK), CHUNK)],
                    sems.at[0],
                )
                copy.start()
                copies.append(copy)

    def clear(i, _):
        acc[0, i] = jnp.zeros((BLOCK, DH), F32)
        acc[1, i] = jnp.zeros((BLOCK, DH), F32)
        return 0

    lax.fori_loop(0, NB, clear, 0)
    for copy in copies:
        copy.wait()

    def span(s, _):
        q = qdo_ref[pl.ds(2 * s, 2), 0:256, :].reshape(ROWS, DH)
        do = qdo_ref[pl.ds(2 * s, 2), 256:512, :].reshape(ROWS, DH)
        q_t[...] = q.T
        do_t[...] = do.T
        dq_t[...] = jnp.zeros((DH, ROWS), F32)
        slot_row = lax.rem(x - s + 4, 4)
        lse = lse_ref[slot_row] * LOG2E
        delta = delta_ref[s]

        def tile(block, start, own):
            keys = kv[0, block, start : start + KEYS, :]
            values = kv[1, block, start : start + KEYS, :]
            scores = jnp.dot(keys, q_t[...], preferred_element_type=F32)
            probs = jnp.exp2(scores * (SCALE * LOG2E) - lse)
            if own:
                key_at = start + lax.broadcasted_iota(jnp.int32, (KEYS, ROWS), 0)
                row = lax.broadcasted_iota(jnp.int32, (KEYS, ROWS), 1)
                query_at = x * CHUNK + (row // 256) * SHARD + lax.rem(row, SHARD)
                probs = jnp.where(key_at <= query_at, probs, 0.0)
            grad_probs = jnp.dot(values, do_t[...], preferred_element_type=F32)
            grad_low = (probs * (grad_probs - delta)).astype(BF)
            acc[1, block, start : start + KEYS, :] += jnp.dot(
                probs.astype(BF), qdo_ref[pl.ds(2 * s, 2), 256:512, :].reshape(ROWS, DH), preferred_element_type=F32
            )
            acc[0, block, start : start + KEYS, :] += jnp.dot(
                grad_low, qdo_ref[pl.ds(2 * s, 2), 0:256, :].reshape(ROWS, DH), preferred_element_type=F32
            )
            dq_t[...] += lax.dot_general(
                keys, grad_low, (((0,), (0,)), ((), ())), preferred_element_type=F32
            )

        own_block = chosen[slot_row, 0]
        for start in range(0, BLOCK, KEYS):
            tile(own_block, start, True)

        def slot(r, _):
            block = chosen[slot_row, r]

            @pl.when(block >= 0)
            def _():
                for start in range(0, BLOCK, KEYS):
                    tile(block, start, False)

            return 0

        lax.fori_loop(1, TOPK, slot, 0)
        dq = (dq_t[...] * SCALE).T.astype(BF)
        dq_ref[pl.ds(2 * s, 2)] = dq.reshape(2, 256, DH)
        return 0

    lax.fori_loop(0, 4, span, 0)

    for which, near, far in ((core, mine_near, mine_far), (1 - core, theirs_near, theirs_far)):
        factor = jnp.where(which == 0, SCALE, 1.0).astype(F32)
        for i1 in range(4):
            for i2 in range(4):
                xb, yb = place(which, OFFSETS[i1], OFFSETS[i2])
                piece = acc[which, pl.ds(yb * 8, 8), pl.ds(pl.multiple_of(xb * CHUNK, CHUNK), CHUNK), :]
                piece = (piece * factor).astype(BF)
                if i1 == 3:
                    far[pl.ds(i2 * 8, 8)] = piece
                else:
                    near[pl.ds((i1 * 4 + i2) * 8, 8)] = piece


def attend(meta, chosen, lse, delta, qdo, mine, other):
    vmem = pl.BlockSpec(memory_space=pltpu.VMEM)
    smem = pl.BlockSpec(memory_space=pltpu.SMEM)
    hbm = pl.BlockSpec(memory_space=pl.ANY)
    shape = jax.ShapeDtypeStruct
    return pl.pallas_call(
        kernel,
        out_shape=(
            shape((32, CHUNK, DH), BF),
            shape((96, CHUNK, DH), BF),
            shape((32, CHUNK, DH), BF),
            shape((96, CHUNK, DH), BF),
            shape((8, 256, DH), BF),
        ),
        in_specs=[smem, smem, vmem, vmem, vmem] + [hbm] * 8,
        out_specs=(vmem,) * 5,
        scratch_shapes=[
            pltpu.VMEM((2, NB, BLOCK, DH), BF),
            pltpu.VMEM((2, NB, BLOCK, DH), F32),
            pltpu.VMEM((DH, ROWS), BF),
            pltpu.VMEM((DH, ROWS), BF),
            pltpu.VMEM((DH, ROWS), F32),
            pltpu.SemaphoreType.DMA((1,)),
        ],
        compiler_params=pltpu.CompilerParams(vmem_limit_bytes=56 * 1024 * 1024),
        cost_estimate=pl.CostEstimate(flops=20 * 10**9, bytes_accessed=20 * 2**20, transcendentals=0),
        name="attend",
    )(meta, chosen, lse, delta, qdo, *mine, *other)


def by_group(array):
    return array.reshape(SHARD, GROUPS, -1, DH).transpose(1, 2, 0, 3)


def from_groups(array):
    return array.transpose(2, 0, 1, 3).reshape(SHARD, -1)


def split_three(array):
    high = lax.reduce_precision(array, 8, 7)
    rest = array - high
    middle = lax.reduce_precision(rest, 8, 7)
    low = rest - middle
    return jnp.stack([high.astype(BF), middle.astype(BF), low.astype(BF)], axis=1)


def shards(queries, key_states, value_states, outputs, out_grad, log_sums, selected):
    x, y, c = lax.axis_index("x"), lax.axis_index("y"), lax.axis_index("c")
    meta = jnp.stack([x, y, c]).astype(jnp.int32)

    keys, values = by_group(key_states), by_group(value_states)
    kv_send = jnp.stack([keys, values], axis=1).reshape(4, 2, 2, SHARD, DH).transpose(0, 2, 1, 3, 4)
    kv_own = lax.all_to_all(kv_send.reshape(16, SHARD, DH), ZCH, split_axis=0, concat_axis=0, tiled=True)
    mine, other = spread(kv_own.reshape(1024, DH))
    mine = [m.reshape(32, CHUNK, DH) for m in mine]
    other = [m.reshape(32, CHUNK, DH) for m in other]

    lse_send = log_sums.reshape(4, 2, SHARD, HQG).transpose(0, 1, 3, 2).reshape(4, ROWS)
    chosen_send = jnp.broadcast_to(selected.reshape(1, TOPK).astype(F32), (4, TOPK))
    small = jnp.concatenate([lse_send, jnp.pad(chosen_send, ((0, 0), (0, 128 - TOPK)))], axis=1)
    z = lax.axis_index("z")
    pieces = []
    for d in range(4):
        piece = lax.dynamic_index_in_dim(small, lax.rem(z + d, 4), 0, keepdims=False)
        pairs = [(zl * 4 + xh, xh * 4 + (zl + d) % 4) for zl in range(4) for xh in range(4)]
        pieces.append(lax.ppermute(piece, ("z", "x"), pairs))
    small = jnp.stack(pieces)
    lse = small[:, :ROWS].reshape(4, 1, ROWS)
    chosen = small[:, ROWS : ROWS + TOPK].astype(jnp.int32)

    delta = jnp.sum(
        (out_grad.astype(F32) * outputs.astype(F32)).reshape(SHARD, GROUPS * HQG, DH), axis=-1
    )
    delta = delta.T.reshape(GROUPS, HQG * SHARD)
    delta_rows = jnp.pad(split_three(delta).reshape(GROUPS, 6, DH), ((0, 0), (0, 10), (0, 0)))
    qdo_send = jnp.concatenate(
        [by_group(queries).reshape(GROUPS, 256, DH), by_group(out_grad).reshape(GROUPS, 256, DH), delta_rows],
        axis=1,
    )
    qdo = lax.all_to_all(qdo_send, ZH, split_axis=0, concat_axis=0, tiled=True)
    delta = jnp.sum(qdo[:, 512:518, :].reshape(8, 3, 256).astype(F32), axis=1).reshape(4, 1, ROWS)

    theirs_far, theirs_near, mine_far, mine_near, dq = attend(meta, chosen, lse, delta, qdo, mine, other)
    flat = lambda a: a.reshape(-1, DH)
    kv_grad = gather_sums(flat(theirs_far), flat(theirs_near), flat(mine_far), flat(mine_near))
    query_grad = lax.all_to_all(dq, ZH, split_axis=0, concat_axis=0, tiled=True)
    kv_grad = lax.all_to_all(kv_grad.reshape(16, SHARD, DH), ZCH, split_axis=0, concat_axis=0, tiled=True)
    kv_grad = kv_grad.reshape(4, 2, 2, SHARD, DH)
    return (
        from_groups(query_grad.reshape(GROUPS, HQG, SHARD, DH)),
        from_groups(kv_grad[:, 0].reshape(GROUPS, 1, SHARD, DH)),
        from_groups(kv_grad[:, 1].reshape(GROUPS, 1, SHARD, DH)),
    )


def solution(mesh):
    wide = Mesh(mesh.devices.reshape(4, 4, 2, 4, 2), ("y", "z", "c", "x", "h"))
    rows = P(("y", "z", "c", "x", "h"), None)
    return jax.shard_map(
        shards,
        mesh=wide,
        in_specs=(
            rows,
            rows,
            rows,
            rows,
            rows,
            P(("y", "z", "c"), ("x", "h")),
            P(("y", "z", "c"), ("x", "h"), None),
        ),
        out_specs=(rows, rows, rows),
        check_vma=False,
    )
```

time: 639 us -> 207 us (0.32)
  waiting for transfers between devices: 416 us -> 97.1 us
  matrix products: 46.6 us -> 0 us
  blocking collectives: 34 us -> 0 us
  local copies, waits for them, and re-layouts: 42.8 us -> 9.04 us
  Pallas kernels: 0 us -> 23.2 us
  starting transfers between devices: 44 us -> 66.9 us
  between operations: 19 us -> 1.03 us
  other arithmetic: 24.6 us -> 7.44 us
  loops' own time: 10.5 us -> 0 us
    reduce_scatter x2 -> x0, waiting for transfers between devices: 299 us -> none  [the longest x1 151 us: shards(): lax.psum_scatter(value_dense, 'ctx', scatter_dimension=0, tiled=True)]
    all_gather x2 -> x0, waiting for transfers between devices: 81.6 us -> none  [the longest x1 78.1 us: shards(): lax.all_gather(value_heads, 'ctx', axis=0, tiled=True)]
    ppermute x0 -> x24, waiting for transfers between devices: none -> 75.3 us  [the longest x14 54.4 us: shift(): return lax.ppermute(array, PLANE, pairs)]
    dot_general x20 -> x0, matrix products: 46.6 us -> none  [the longest x4 13.9 us: per_pair(): jnp.einsum('qd,kd->qk', query_one, keys_here, preferred_element_type=jnp....]
    ppermute x0 -> x24, starting transfers between devices: none -> 45.6 us  [the longest x14 36.6 us: shift(): return lax.ppermute(array, PLANE, pairs)]
    all_to_all x2 -> x0, blocking collectives: 34 us -> none  [the longest x1 20.3 us: shards(): lax.all_to_all(key_states, 'head', split_axis=1, concat_axis=0, tiled=True)]
    pallas_call x0 -> x1, Pallas kernels: none -> 23.2 us  [attend(): pl.pallas_call(kernel, out_shape=(shape((32, CHUNK, DH), BF), shape((96,...]
    all_to_all x6 -> x4, starting transfers between devices: 43.9 us -> 21.3 us  [the longest x1 8.57 us: shards(): lax.all_to_all(kv_send.reshape(16, SHARD, DH), ZCH, split_axis=0, concat_...]
  transfers between devices with their start and end apart: 10 -> 28, of which waited for: 7 -> 20; matrix products, arithmetic and copies ran while one was open for 4% -> 5% of each run, Pallas kernels for 0% -> 0%
where the time goes in v1:
time: 207 us; the launch traced here: 205 us
  waiting for transfers between devices  97.1 us (47%)
  starting transfers between devices  66.9 us (32%)
  Pallas kernels  23.2 us (11%)
  local copies, waits for them, and re-layouts  9.04 us (4%)
  other arithmetic  7.44 us (4%)
    ppermute x14, waiting for transfers between devices, shift(): return lax.ppermute(array, PLANE, pairs)  54.4 us
    ppermute x14, starting transfers between devices, shift(): return lax.ppermute(array, PLANE, pairs)  36.6 us
    pallas_call x1, Pallas kernels, attend(): pl.pallas_call(kernel, out_shape=(shape((32, CHUNK, DH), BF), shape((96,...  23.2 us
    ppermute x4, waiting for transfers between devices, shards(): pieces.append(lax.ppermute(piece, ('z', 'x'), pairs))  14 us
    all_to_all x1, waiting for transfers between devices, shards(): lax.all_to_all(kv_grad.reshape(16, SHARD, DH), ZCH, split_axis=0, concat_...  10.7 us
    all_to_all x1, waiting for transfers between devices, shards(): lax.all_to_all(kv_send.reshape(16, SHARD, DH), ZCH, split_axis=0, concat_...  10.3 us
    all_to_all x1, starting transfers between devices, shards(): lax.all_to_all(kv_send.reshape(16, SHARD, DH), ZCH, split_axis=0, concat_...  8.57 us
    ppermute x4, starting transfers between devices, shards(): pieces.append(lax.ppermute(piece, ('z', 'x'), pairs))  8.25 us
  transfers between devices with their start and end apart: 28, of which 20 were waited for; matrix products, arithmetic and copies ran while one was open for 5% of the time, Pallas kernels for 0%

profile of v1, /device:TPU:2, one launch (start us, length us, event | category | flops | bytes accessed | tf_op | source)
XLA Modules:
  0.0 204.7 jit_solution(10857665490798877845)
XLA Ops:
  3.7 8.6 %all-to-all-start.1 = ((bf16[16,64,128]{2,1,0:T(8,128)(2,1)}), bf16[16,64,128]{2,1,0:T(8,128)(2,1)S(1)}, u32[]{:S(2)}, u32[]{:S(2)}) async-start(bf16[16,64,128]{2,1,0:T(8,128)(2,1)} %bitcast.15), calls=%async_computation.1 | async-start | bytes 524288 | tf_op jit(solution)/shard_map/all_to_all | solution.py:241
  14.3 10.3 %all-to-all-done.1 = bf16[16,64,128]{2,1,0:T(8,128)(2,1)S(1)} async-done(((bf16[16,64,128]{2,1,0:T(8,128)(2,1)}), bf16[16,64,128]{2,1,0:T(8,128)(2,1)S(1)}, u32[]{:S(2)}, u32[]{:S(2)}) %all-to-all-start.1) | async-done | bytes 262176 | tf_op jit(solution)/shard_map/all_to_all | solution.py:241
  28.8 3.8 %collective-permute-done.6 = bf16[1024,128]{1,0:T(8,128)(2,1)S(1)} collective-permute-done((bf16[1024,128]{1,0:T(8,128)(2,1)S(1)}, bf16[1024,128]{1,0:T(8,128)(2,1)S(1)}, u32[]{:S(2)}, u32[]{:S(2)}) %collective-permute-start.6) | collective-permute-done | bytes 262176 | tf_op jit(solution)/shard_map/ppermute | solution.py:42
  32.6 2.8 %collective-permute-done.5 = bf16[1024,128]{1,0:T(8,128)(2,1)S(1)} collective-permute-done((bf16[1024,128]{1,0:T(8,128)(2,1)S(1)}, bf16[1024,128]{1,0:T(8,128)(2,1)S(1)}, u32[]{:S(2)}, u32[]{:S(2)}) %collective-permute-start.5) | collective-permute-done | bytes 262176 | tf_op jit(solution)/shard_map/ppermute | solution.py:42
  35.4 3.3 %collective-permute-start.9 = (bf16[4096,128]{1,0:T(8,128)(2,1)S(1)}, bf16[4096,128]{1,0:T(8,128)(2,1)}, u32[]{:S(2)}, u32[]{:S(2)}) collective-permute-start(bf16[4096,128]{1,0:T(8,128)(2,1)S(1)} %pad_maximum_fusion), channel_id=1, source_target_pairs={{0,128},{2,130},{4,132},{6,134},{8,12},{10,14},{12,8},{14,10},{64,... | collective-permute-start | bytes 3145736 | tf_op jit(solution)/shard_map/ppermute | solution.py:42
  43.0 3.6 %all-to-all-start = ((bf16[8,528,128]{2,1,0:T(8,128)(2,1)}), bf16[8,528,128]{2,1,0:T(8,128)(2,1)S(1)}, u32[]{:S(2)}, u32[]{:S(2)}) async-start(bf16[8,528,128]{2,1,0:T(8,128)(2,1)} %fusion.4), calls=%async_computation | async-start | bytes 2162688 | tf_op jit(solution)/shard_map/all_to_all | solution.py:268
  46.9 5.2 %collective-permute-done.9 = bf16[4096,128]{1,0:T(8,128)(2,1)} collective-permute-done((bf16[4096,128]{1,0:T(8,128)(2,1)S(1)}, bf16[4096,128]{1,0:T(8,128)(2,1)}, u32[]{:S(2)}, u32[]{:S(2)}) %collective-permute-start.9) | collective-permute-done | bytes 1048608 | tf_op jit(solution)/shard_map/ppermute | solution.py:42
  52.1 11.1 %collective-permute-done.8 = bf16[4096,128]{1,0:T(8,128)(2,1)} collective-permute-done((bf16[4096,128]{1,0:T(8,128)(2,1)S(1)}, bf16[4096,128]{1,0:T(8,128)(2,1)}, u32[]{:S(2)}, u32[]{:S(2)}) %collective-permute-start.8) | collective-permute-done | bytes 1048608 | tf_op jit(solution)/shard_map/ppermute | solution.py:42
  63.8 2.8 %collective-permute-start = (f32[640]{0:T(1024)S(1)}, f32[640]{0:T(1024)S(1)}, u32[]{:S(2)}, u32[]{:S(2)}) collective-permute-start(f32[640]{0:T(1024)S(1)} %get-tuple-element.13), channel_id=1, source_target_pairs={{0,0},{2,16},{4,32},{6,48},{16,2},{18,18},{20,34},{22,50},{32,4},{... | collective-permute-start | bytes 7688 | tf_op jit(solution)/shard_map/ppermute | solution.py:254
  66.6 3.8 %collective-permute-done = f32[640]{0:T(1024)S(1)} collective-permute-done((f32[640]{0:T(1024)S(1)}, f32[640]{0:T(1024)S(1)}, u32[]{:S(2)}, u32[]{:S(2)}) %collective-permute-start) | collective-permute-done | bytes 2592 | tf_op jit(solution)/shard_map/ppermute | solution.py:254
  70.5 4.9 %collective-permute-start.3 = (f32[640]{0:T(1024)S(1)}, f32[640]{0:T(1024)S(1)}, u32[]{:S(2)}, u32[]{:S(2)}) collective-permute-start(f32[640]{0:T(1024)S(1)} %get-tuple-element.14), channel_id=1, source_target_pairs={{0,6},{2,22},{4,38},{6,54},{16,0},{18,16},{20,32},{22,48},{32,2},{... | collective-permute-start | bytes 7688 | tf_op jit(solution)/shard_map/ppermute | solution.py:254
  76.9 6.1 %collective-permute-done.2 = f32[640]{0:T(1024)S(1)} collective-permute-done((f32[640]{0:T(1024)S(1)}, f32[640]{0:T(1024)S(1)}, u32[]{:S(2)}, u32[]{:S(2)}) %collective-permute-start.2) | collective-permute-done | bytes 2592 | tf_op jit(solution)/shard_map/ppermute | solution.py:254
  83.9 2.8 %collective-permute-done.1 = f32[640]{0:T(1024)S(1)} collective-permute-done((f32[640]{0:T(1024)S(1)}, f32[640]{0:T(1024)S(1)}, u32[]{:S(2)}, u32[]{:S(2)}) %collective-permute-start.1) | collective-permute-done | bytes 2592 | tf_op jit(solution)/shard_map/ppermute | solution.py:254
  88.9 23.2 %attend.1 = (bf16[32,128,128]{2,1,0:T(8,128)(2,1)}, bf16[96,128,128]{2,1,0:T(8,128)(2,1)}, bf16[32,128,128]{2,1,0:T(8,128)(2,1)}, bf16[96,128,128]{2,1,0:T(8,128)(2,1)}, bf16[8,256,128]{2,1,0:T(8,128)(2,1)}) custom-call(s32[3]{0:T(128)} %pad_add_fusion.meta, s32[4,8]{1,0:T(4,128)} %maximum_convert_fusion.chosen, f32[4,1,512]{2,1,0:T(1,128)} %reshape.184.lse_ref, ...), custom_call_target="tpu_custom_call" | custom-call | flops 20000000000 | bytes 20971520 | tf_op jit(solution)/shard_map/attend/pallas_call | solution.py:194
  112.6 6.9 %collective-permute-done.15 = bf16[4096,128]{1,0:T(8,128)(2,1)S(1)} collective-permute-done((bf16[4096,128]{1,0:T(8,128)(2,1)}, bf16[4096,128]{1,0:T(8,128)(2,1)S(1)}, u32[]{:S(2)}, u32[]{:S(2)}) %collective-permute-start.15) | collective-permute-done | bytes 1048608 | tf_op jit(solution)/shard_map/ppermute | solution.py:46
  121.2 5.5 %collective-permute-start.16 = (bf16[2048,128]{1,0:T(8,128)(2,1)S(1)}, bf16[2048,128]{1,0:T(8,128)(2,1)S(1)}, u32[]{:S(2)}, u32[]{:S(2)}) collective-permute-start(bf16[2048,128]{1,0:T(8,128)(2,1)S(1)} %get-tuple-element.33), channel_id=1, source_target_pairs={{0,2},{2,4},{4,6},{6,0},{8,72},{10,74},{12,76},{14,78},{64,66},{66... | collective-permute-start | bytes 1572872 | tf_op jit(solution)/shard_map/ppermute | solution.py:42
  127.0 6.4 %collective-permute-done.16 = bf16[2048,128]{1,0:T(8,128)(2,1)S(1)} collective-permute-done((bf16[2048,128]{1,0:T(8,128)(2,1)S(1)}, bf16[2048,128]{1,0:T(8,128)(2,1)S(1)}, u32[]{:S(2)}, u32[]{:S(2)}) %collective-permute-start.16) | collective-permute-done | bytes 524320 | tf_op jit(solution)/shard_map/ppermute | solution.py:42
  139.3 12.5 %collective-permute-done.19 = bf16[4096,128]{1,0:T(8,128)(2,1)S(1)} collective-permute-done((bf16[4096,128]{1,0:T(8,128)(2,1)S(1)}, bf16[4096,128]{1,0:T(8,128)(2,1)S(1)}, u32[]{:S(2)}, u32[]{:S(2)}) %collective-permute-start.19) | collective-permute-done | bytes 1048608 | tf_op jit(solution)/shard_map/ppermute | solution.py:42
  154.0 15.4 %collective-permute-start.20 = (bf16[512,128]{1,0:T(8,128)(2,1)S(1)}, bf16[512,128]{1,0:T(8,128)(2,1)S(1)}, u32[]{:S(2)}, u32[]{:S(2)}) collective-permute-start(bf16[512,128]{1,0:T(8,128)(2,1)S(1)} %get-tuple-element.29), channel_id=1, source_target_pairs={{0,64},{2,66},{4,68},{6,70},{8,10},{10,12},{12,14},{14,8},{64,128}... | collective-permute-start | bytes 393224 | tf_op jit(solution)/shard_map/ppermute | solution.py:42
  170.1 3.5 %all-to-all-start.2 = ((bf16[8,256,128]{2,1,0:T(8,128)(2,1)}), bf16[8,256,128]{2,1,0:T(8,128)(2,1)S(1)}, u32[]{:S(2)}, u32[]{:S(2)}) async-start(bf16[8,256,128]{2,1,0:T(8,128)(2,1)} %get-tuple-element.8), calls=%async_computation.2 | async-start | bytes 1048576 | tf_op jit(solution)/shard_map/all_to_all | solution.py:274
  176.7 4.2 %collective-permute-done.23 = bf16[1024,128]{1,0:T(8,128)(2,1)S(1)} collective-permute-done((bf16[1024,128]{1,0:T(8,128)(2,1)S(1)}, bf16[1024,128]{1,0:T(8,128)(2,1)S(1)}, u32[]{:S(2)}, u32[]{:S(2)}) %collective-permute-start.23) | collective-permute-done | bytes 262176 | tf_op jit(solution)/shard_map/ppermute | solution.py:42
  181.0 3.1 %collective-permute-done.21 = bf16[1024,128]{1,0:T(8,128)(2,1)S(1)} collective-permute-done((bf16[1024,128]{1,0:T(8,128)(2,1)S(1)}, bf16[1024,128]{1,0:T(8,128)(2,1)S(1)}, u32[]{:S(2)}, u32[]{:S(2)}) %collective-permute-start.21) | collective-permute-done | bytes 262176 | tf_op jit(solution)/shard_map/ppermute | solution.py:42
  185.7 5.6 %all-to-all-start.3 = ((bf16[16,64,128]{2,1,0:T(8,128)(2,1)}), bf16[16,64,128]{2,1,0:T(8,128)(2,1)S(1)}, u32[]{:S(2)}, u32[]{:S(2)}) async-start(bf16[16,64,128]{2,1,0:T(8,128)(2,1)} %bitcast.35), calls=%async_computation.3 | async-start | bytes 524288 | tf_op jit(solution)/shard_map/all_to_all | solution.py:275
  193.0 10.7 %all-to-all-done.3 = bf16[16,64,128]{2,1,0:T(8,128)(2,1)S(1)} async-done(((bf16[16,64,128]{2,1,0:T(8,128)(2,1)}), bf16[16,64,128]{2,1,0:T(8,128)(2,1)S(1)}, u32[]{:S(2)}, u32[]{:S(2)}) %all-to-all-start.3) | async-done | bytes 262176 | tf_op jit(solution)/shard_map/all_to_all | solution.py:275
  (106 shorter events, 37.5 us)
Async XLA Ops:
  3.7 20.9 %all-to-all-start.1 = ((bf16[16,64,128]{2,1,0:T(8,128)(2,1)}), bf16[16,64,128]{2,1,0:T(8,128)(2,1)S(1)}, u32[]{:S(2)}, u32[]{:S(2)}) async-start(bf16[16,64,128]{2,1,0:T(8,128)(2,1)} %bitcast.15), calls=%async_computation.1 | async-start | bytes 524288 | tf_op jit(solution)/shard_map/all_to_all | solution.py:241
  24.6 8.0 %collective-permute-start.6 = (bf16[1024,128]{1,0:T(8,128)(2,1)S(1)}, bf16[1024,128]{1,0:T(8,128)(2,1)S(1)}, u32[]{:S(2)}, u32[]{:S(2)}) collective-permute-start(bf16[1024,128]{1,0:T(8,128)(2,1)S(1)} %bitcast.96), channel_id=1, source_target_pairs={{0,4},{2,6},{4,0},{6,2},{8,136},{10,138},{12,140},{14,142},{64,68}... | collective-permute-start | bytes 786440 | tf_op jit(solution)/shard_map/ppermute | solution.py:42
  26.7 8.6 %collective-permute-start.5 = (bf16[1024,128]{1,0:T(8,128)(2,1)S(1)}, bf16[1024,128]{1,0:T(8,128)(2,1)S(1)}, u32[]{:S(2)}, u32[]{:S(2)}) collective-permute-start(bf16[1024,128]{1,0:T(8,128)(2,1)S(1)} %bitcast.97), channel_id=1, source_target_pairs={{0,2},{2,4},{4,6},{6,0},{8,72},{10,74},{12,76},{14,78},{64,66},{66... | collective-permute-start | bytes 786440 | tf_op jit(solution)/shard_map/ppermute | solution.py:42
  26.7 8.6 %collective-permute-start.4 = (bf16[1024,128]{1,0:T(8,128)(2,1)S(1)}, bf16[1024,128]{1,0:T(8,128)(2,1)S(1)}, u32[]{:S(2)}, u32[]{:S(2)}) collective-permute-start(bf16[1024,128]{1,0:T(8,128)(2,1)S(1)} %bitcast.98), channel_id=1, source_target_pairs={{0,6},{2,0},{4,2},{6,4},{8,200},{10,202},{12,204},{14,206},{64,70}... | collective-permute-start | bytes 786440 | tf_op jit(solution)/shard_map/ppermute | solution.py:42
  35.4 16.6 %collective-permute-start.9 = (bf16[4096,128]{1,0:T(8,128)(2,1)S(1)}, bf16[4096,128]{1,0:T(8,128)(2,1)}, u32[]{:S(2)}, u32[]{:S(2)}) collective-permute-start(bf16[4096,128]{1,0:T(8,128)(2,1)S(1)} %pad_maximum_fusion), channel_id=1, source_target_pairs={{0,128},{2,130},{4,132},{6,134},{8,12},{10,14},{12,8},{14,10},{64,... | collective-permute-start | bytes 3145736 | tf_op jit(solution)/shard_map/ppermute | solution.py:42
  38.7 24.4 %collective-permute-start.8 = (bf16[4096,128]{1,0:T(8,128)(2,1)S(1)}, bf16[4096,128]{1,0:T(8,128)(2,1)}, u32[]{:S(2)}, u32[]{:S(2)}) collective-permute-start(bf16[4096,128]{1,0:T(8,128)(2,1)S(1)} %pad_maximum_fusion), channel_id=1, source_target_pairs={{0,64},{2,66},{4,68},{6,70},{8,10},{10,12},{12,14},{14,8},{64,128}... | collective-permute-start | bytes 3145736 | tf_op jit(solution)/shard_map/ppermute | solution.py:42
  39.4 24.2 %collective-permute-start.7 = (bf16[4096,128]{1,0:T(8,128)(2,1)S(1)}, bf16[4096,128]{1,0:T(8,128)(2,1)}, u32[]{:S(2)}, u32[]{:S(2)}) collective-permute-start(bf16[4096,128]{1,0:T(8,128)(2,1)S(1)} %pad_maximum_fusion), channel_id=1, source_target_pairs={{0,192},{2,194},{4,196},{6,198},{8,14},{10,8},{12,10},{14,12},{64,... | collective-permute-start | bytes 3145736 | tf_op jit(solution)/shard_map/ppermute | solution.py:42
  43.0 44.8 %all-to-all-start = ((bf16[8,528,128]{2,1,0:T(8,128)(2,1)}), bf16[8,528,128]{2,1,0:T(8,128)(2,1)S(1)}, u32[]{:S(2)}, u32[]{:S(2)}) async-start(bf16[8,528,128]{2,1,0:T(8,128)(2,1)} %fusion.4), calls=%async_computation | async-start | bytes 2162688 | tf_op jit(solution)/shard_map/all_to_all | solution.py:268
  46.8 41.8 %collective-permute-start.10 = (bf16[4096,128]{1,0:T(8,128)(2,1)S(1)}, bf16[4096,128]{1,0:T(8,128)(2,1)}, u32[]{:S(2)}, u32[]{:S(2)}) collective-permute-start(bf16[4096,128]{1,0:T(8,128)(2,1)S(1)} %pad_maximum_fusion), channel_id=1, source_target_pairs={{0,8},{8,0},{1,9},{9,1},{2,10},{10,2},{3,11},{11,3},{4,12},{12,4},... | collective-permute-start | bytes 3145736 | tf_op jit(solution)/shard_map/ppermute | solution.py:46
  52.0 36.6 %collective-permute-start.13 = (bf16[4096,128]{1,0:T(8,128)(2,1)}, bf16[4096,128]{1,0:T(8,128)(2,1)}, u32[]{:S(2)}, u32[]{:S(2)}) collective-permute-start(bf16[4096,128]{1,0:T(8,128)(2,1)} %collective-permute-done.9), channel_id=1, source_target_pairs={{0,8},{8,0},{1,9},{9,1},{2,10},{10,2},{3,11},{11,3},{4,12},{12,4},... | collective-permute-start | bytes 3145736 | tf_op jit(solution)/shard_map/ppermute | solution.py:46
  63.2 25.5 %collective-permute-start.12 = (bf16[4096,128]{1,0:T(8,128)(2,1)}, bf16[4096,128]{1,0:T(8,128)(2,1)}, u32[]{:S(2)}, u32[]{:S(2)}) collective-permute-start(bf16[4096,128]{1,0:T(8,128)(2,1)} %collective-permute-done.8), channel_id=1, source_target_pairs={{0,8},{8,0},{1,9},{9,1},{2,10},{10,2},{3,11},{11,3},{4,12},{12,4},... | collective-permute-start | bytes 3145736 | tf_op jit(solution)/shard_map/ppermute | solution.py:46
  63.6 25.1 %collective-permute-start.11 = (bf16[4096,128]{1,0:T(8,128)(2,1)}, bf16[4096,128]{1,0:T(8,128)(2,1)}, u32[]{:S(2)}, u32[]{:S(2)}) collective-permute-start(bf16[4096,128]{1,0:T(8,128)(2,1)} %collective-permute-done.7), channel_id=1, source_target_pairs={{0,8},{8,0},{1,9},{9,1},{2,10},{10,2},{3,11},{11,3},{4,12},{12,4},... | collective-permute-start | bytes 3145736 | tf_op jit(solution)/shard_map/ppermute | solution.py:46
  63.8 6.7 %collective-permute-start = (f32[640]{0:T(1024)S(1)}, f32[640]{0:T(1024)S(1)}, u32[]{:S(2)}, u32[]{:S(2)}) collective-permute-start(f32[640]{0:T(1024)S(1)} %get-tuple-element.13), channel_id=1, source_target_pairs={{0,0},{2,16},{4,32},{6,48},{16,2},{18,18},{20,34},{22,50},{32,4},{... | collective-permute-start | bytes 7688 | tf_op jit(solution)/shard_map/ppermute | solution.py:254
  112.0 23.9 %collective-permute-start.14 = (bf16[12288,128]{1,0:T(8,128)(2,1)}, bf16[12288,128]{1,0:T(8,128)(2,1)S(1)}, u32[]{:S(2)}, u32[]{:S(2)}) collective-permute-start(bf16[12288,128]{1,0:T(8,128)(2,1)} %bitcast.108), channel_id=1, source_target_pairs={{0,8},{8,0},{1,9},{9,1},{2,10},{10,2},{3,11},{11,3},{4,12},{12,4},... | collective-permute-start | bytes 9437192 | tf_op jit(solution)/shard_map/ppermute | solution.py:46
  112.1 7.4 %collective-permute-start.15 = (bf16[4096,128]{1,0:T(8,128)(2,1)}, bf16[4096,128]{1,0:T(8,128)(2,1)S(1)}, u32[]{:S(2)}, u32[]{:S(2)}) collective-permute-start(bf16[4096,128]{1,0:T(8,128)(2,1)} %bitcast.109), channel_id=1, source_target_pairs={{0,8},{8,0},{1,9},{9,1},{2,10},{10,2},{3,11},{11,3},{4,12},{12,4},... | collective-permute-start | bytes 3145736 | tf_op jit(solution)/shard_map/ppermute | solution.py:46
  121.2 12.2 %collective-permute-start.16 = (bf16[2048,128]{1,0:T(8,128)(2,1)S(1)}, bf16[2048,128]{1,0:T(8,128)(2,1)S(1)}, u32[]{:S(2)}, u32[]{:S(2)}) collective-permute-start(bf16[2048,128]{1,0:T(8,128)(2,1)S(1)} %get-tuple-element.33), channel_id=1, source_target_pairs={{0,2},{2,4},{4,6},{6,0},{8,72},{10,74},{12,76},{14,78},{64,66},{66... | collective-permute-start | bytes 1572872 | tf_op jit(solution)/shard_map/ppermute | solution.py:42
  126.8 9.2 %collective-permute-start.18 = (bf16[2048,128]{1,0:T(8,128)(2,1)S(1)}, bf16[2048,128]{1,0:T(8,128)(2,1)S(1)}, u32[]{:S(2)}, u32[]{:S(2)}) collective-permute-start(bf16[2048,128]{1,0:T(8,128)(2,1)S(1)} %get-tuple-element.34), channel_id=1, source_target_pairs={{0,6},{2,0},{4,2},{6,4},{8,200},{10,202},{12,204},{14,206},{64,70}... | collective-permute-start | bytes 1572872 | tf_op jit(solution)/shard_map/ppermute | solution.py:42
  136.9 14.9 %collective-permute-start.19 = (bf16[4096,128]{1,0:T(8,128)(2,1)S(1)}, bf16[4096,128]{1,0:T(8,128)(2,1)S(1)}, u32[]{:S(2)}, u32[]{:S(2)}) collective-permute-start(bf16[4096,128]{1,0:T(8,128)(2,1)S(1)} %pad_maximum_fusion.2), channel_id=1, source_target_pairs={{0,6},{2,0},{4,2},{6,4},{8,200},{10,202},{12,204},{14,206},{64,70}... | collective-permute-start | bytes 3145736 | tf_op jit(solution)/shard_map/ppermute | solution.py:42
  137.1 16.2 %collective-permute-start.17 = (bf16[4096,128]{1,0:T(8,128)(2,1)S(1)}, bf16[4096,128]{1,0:T(8,128)(2,1)S(1)}, u32[]{:S(2)}, u32[]{:S(2)}) collective-permute-start(bf16[4096,128]{1,0:T(8,128)(2,1)S(1)} %pad_maximum_fusion.1), channel_id=1, source_target_pairs={{0,2},{2,4},{4,6},{6,0},{8,72},{10,74},{12,76},{14,78},{64,66},{66... | collective-permute-start | bytes 3145736 | tf_op jit(solution)/shard_map/ppermute | solution.py:42
  154.0 19.5 %collective-permute-start.20 = (bf16[512,128]{1,0:T(8,128)(2,1)S(1)}, bf16[512,128]{1,0:T(8,128)(2,1)S(1)}, u32[]{:S(2)}, u32[]{:S(2)}) collective-permute-start(bf16[512,128]{1,0:T(8,128)(2,1)S(1)} %get-tuple-element.29), channel_id=1, source_target_pairs={{0,64},{2,66},{4,68},{6,70},{8,10},{10,12},{12,14},{14,8},{64,128}... | collective-permute-start | bytes 393224 | tf_op jit(solution)/shard_map/ppermute | solution.py:42
  170.1 15.7 %all-to-all-start.2 = ((bf16[8,256,128]{2,1,0:T(8,128)(2,1)}), bf16[8,256,128]{2,1,0:T(8,128)(2,1)S(1)}, u32[]{:S(2)}, u32[]{:S(2)}) async-start(bf16[8,256,128]{2,1,0:T(8,128)(2,1)} %get-tuple-element.8), calls=%async_computation.2 | async-start | bytes 1048576 | tf_op jit(solution)/shard_map/all_to_all | solution.py:274
  174.5 6.4 %collective-permute-start.23 = (bf16[1024,128]{1,0:T(8,128)(2,1)S(1)}, bf16[1024,128]{1,0:T(8,128)(2,1)S(1)}, u32[]{:S(2)}, u32[]{:S(2)}) collective-permute-start(bf16[1024,128]{1,0:T(8,128)(2,1)S(1)} %pad_maximum_fusion.4), channel_id=1, source_target_pairs={{0,192},{2,194},{4,196},{6,198},{8,14},{10,8},{12,10},{14,12},{64,... | collective-permute-start | bytes 786440 | tf_op jit(solution)/shard_map/ppermute | solution.py:42
  176.4 7.7 %collective-permute-start.21 = (bf16[1024,128]{1,0:T(8,128)(2,1)S(1)}, bf16[1024,128]{1,0:T(8,128)(2,1)S(1)}, u32[]{:S(2)}, u32[]{:S(2)}) collective-permute-start(bf16[1024,128]{1,0:T(8,128)(2,1)S(1)} %pad_maximum_fusion.3), channel_id=1, source_target_pairs={{0,64},{2,66},{4,68},{6,70},{8,10},{10,12},{12,14},{14,8},{64,128}... | collective-permute-start | bytes 786440 | tf_op jit(solution)/shard_map/ppermute | solution.py:42
  185.7 17.9 %all-to-all-start.3 = ((bf16[16,64,128]{2,1,0:T(8,128)(2,1)}), bf16[16,64,128]{2,1,0:T(8,128)(2,1)S(1)}, u32[]{:S(2)}, u32[]{:S(2)}) async-start(bf16[16,64,128]{2,1,0:T(8,128)(2,1)} %bitcast.35), calls=%async_computation.3 | async-start | bytes 524288 | tf_op jit(solution)/shard_map/all_to_all | solution.py:275
  (12 other events, 92.3 us)

commit v2 on v1

v2 whole, which is shorter than its diff:
```python
import functools

import jax
import jax.numpy as jnp
from jax import lax
from jax.experimental import pallas as pl
from jax.experimental.pallas import tpu as pltpu
from jax.sharding import Mesh, PartitionSpec as P

DH = 128
HQG = 4
BLOCK = 512
TOPK = 8
GROUPS = 8
HELD = 16
EXTRA = 32
SHARD = 64
CHUNK = 128
ROWS = 512
UNROLL = 2
SCALE = DH ** (-0.5)
LOG2E = 1.4426950408889634
ZH = ("z", "h")
PLANE = ("y", "c", "x")
OFFSETS = (0, 1, -1, 2)
BF = jnp.bfloat16
F32 = jnp.float32


def plane_index(y, c, x):
    return ((y % 4) * 2 + c) * 4 + (x % 4)


def shift(array, phase, distance):
    pairs = []
    for y in range(4):
        for c in range(2):
            for x in range(4):
                along_x = (c == 0) == (phase == 0)
                target = plane_index(y, c, x + distance) if along_x else plane_index(y + distance, c, x)
                pairs.append((plane_index(y, c, x), target))
    return lax.ppermute(array, PLANE, pairs)


def swap(array):
    return lax.ppermute(array, "c", [(0, 1), (1, 0)])


def tie(first, *rest):
    return lax.optimization_barrier((first, *rest))


def after(array, *others):
    return lax.optimization_barrier((array, *others))[0]


def round_the_ring(array, phase):
    return [shift(array, phase, -d) for d in OFFSETS[1:]]


def kernel(
    meta, chosen, lse_ref, delta_ref, qdo_own, qdo_other, w0, w1, w2, w3,
    own_ref, plus_ref, minus_ref, far_ref, dq_own, dq_other,
    qdo, kv, acc, dq_t, items, sems,
):
    x, y, core = meta[0], meta[1], meta[2]

    def place(d1, d2):
        on_x = core == 0
        return (
            lax.rem(x + jnp.where(on_x, d1, d2) + 4, 4),
            lax.rem(y + jnp.where(on_x, d2, d1) + 4, 4),
        )

    copies = [
        pltpu.make_async_copy(ref, qdo.at[i], sems.at[0]) for i, ref in enumerate((qdo_own, qdo_other))
    ]
    for i2, ref in enumerate((w0, w1, w2, w3)):
        for i1 in range(4):
            xb, yb = place(OFFSETS[i1], OFFSETS[i2])
            copies.append(pltpu.make_async_copy(ref.at[i1], kv.at[pl.ds(yb * 4, 4), xb], sems.at[0]))
    for copy in copies:
        copy.start()

    def clear(i, _):
        acc[i] = jnp.zeros(acc.shape[1:], F32)
        return 0

    lax.fori_loop(0, HELD, clear, 0)
    dq_t[...] = jnp.zeros_like(dq_t)

    def span_q(e):
        return qdo[e // 4, pl.ds(2 * lax.rem(e, 4), 2), 0:256, :].reshape(ROWS, DH)

    def span_do(e):
        return qdo[e // 4, pl.ds(2 * lax.rem(e, 4), 2), 256:512, :].reshape(ROWS, DH)

    def listing(i, count):
        e = i // (TOPK - 1)
        block = chosen[e, 1 + lax.rem(i, TOPK - 1)]
        take = jnp.logical_and(block >= 0, lax.rem(block, 2) == core)
        items[count] = e * 64 + block // 2
        return count + take.astype(jnp.int32)

    count = lax.fori_loop(0, 8 * (TOPK - 1), listing, jnp.int32(0))
    for i in range(UNROLL):
        items[count + i] = jnp.int32(0)
    for copy in copies:
        copy.wait()

    def item(e, block, own, live):
        keys = kv[block, :, :, 0].reshape(BLOCK, DH)
        values = kv[block, :, :, 1].reshape(BLOCK, DH)
        q, do = span_q(e), span_do(e)
        lse = lse_ref[e] * LOG2E
        if live is not None:
            lse = lse + jnp.where(live, 0.0, 1e30)
        last = (((1,), (1,)), ((), ()))
        scores = lax.dot_general(keys, q, last, preferred_element_type=F32)
        probs = jnp.exp2(scores * (SCALE * LOG2E) - lse)
        if own:
            key_at = lax.broadcasted_iota(jnp.int32, (BLOCK, ROWS), 0)
            row = lax.broadcasted_iota(jnp.int32, (BLOCK, ROWS), 1)
            query_at = x * CHUNK + (row // 256) * SHARD + lax.rem(row, SHARD)
            probs = jnp.where(key_at <= query_at, probs, 0.0)
        grad_probs = lax.dot_general(values, do, last, preferred_element_type=F32)
        grad_low = (probs * (grad_probs - delta_ref[e])).astype(BF)
        split = lambda a: a.reshape(4, 2, SHARD, DH)
        acc[block, :, :, 1] += split(jnp.dot(probs.astype(BF), do, preferred_element_type=F32))
        acc[block, :, :, 0] += split(jnp.dot(grad_low, q, preferred_element_type=F32))
        dq_t[e] += lax.dot_general(keys, grad_low, (((0,), (0,)), ((), ())), preferred_element_type=F32)

    for s in range(4):
        item(s, chosen[s, 0] // 2, True, None)

    def some(i, _):
        for u in range(UNROLL):
            at = i * UNROLL + u
            code = items[at]
            item(code // 64, lax.rem(code, 64), False, None if u == 0 else at < count)
        return 0

    lax.fori_loop(0, (count + UNROLL - 1) // UNROLL, some, 0)

    for i1, ref in ((3, far_ref), (1, plus_ref), (2, minus_ref), (0, own_ref)):
        for i2 in range(4):
            xb, yb = place(OFFSETS[i1], OFFSETS[i2])
            piece = acc[pl.ds(yb * 4, 4), xb]
            ref[i2, :, :, 0] = (piece[:, :, 0] * SCALE).astype(ref.dtype)
            ref[i2, :, :, 1] = piece[:, :, 1].astype(ref.dtype)

    def finish(s, _):
        dq_own[pl.ds(2 * s, 2)] = (dq_t[s] * SCALE).T.reshape(2, 256, DH)
        dq_other[pl.ds(2 * s, 2)] = (dq_t[s + 4] * SCALE).T.reshape(2, 256, DH)
        return 0

    lax.fori_loop(0, 4, finish, 0)


def attend(meta, chosen, lse, delta, qdo_own, qdo_other, rows):
    vmem = pl.BlockSpec(memory_space=pltpu.VMEM)
    smem = pl.BlockSpec(memory_space=pltpu.SMEM)
    hbm = pl.BlockSpec(memory_space=pl.ANY)
    shape = jax.ShapeDtypeStruct
    chunk = (4, 4, 2, 2, SHARD, DH)
    return pl.pallas_call(
        kernel,
        out_shape=(shape(chunk, F32),) + (shape(chunk, BF),) * 3 + (shape((8, 256, DH), F32),) * 2,
        in_specs=[smem, smem, vmem, vmem] + [hbm] * 6,
        out_specs=(vmem,) * 6,
        scratch_shapes=[
            pltpu.VMEM((2, GROUPS, ROWS + EXTRA, DH), BF),
            pltpu.VMEM((HELD, 4, 2, 2, SHARD, DH), BF),
            pltpu.VMEM((HELD, 4, 2, 2, SHARD, DH), F32),
            pltpu.VMEM((8, DH, ROWS), F32),
            pltpu.SMEM((64,), jnp.int32),
            pltpu.SemaphoreType.DMA((1,)),
        ],
        compiler_params=pltpu.CompilerParams(vmem_limit_bytes=56 * 1024 * 1024),
        cost_estimate=pl.CostEstimate(flops=20 * 10**9, bytes_accessed=20 * 2**20, transcendentals=0),
        name="attend",
    )(meta, chosen, lse, delta, qdo_own, qdo_other, *rows)


def by_group(array):
    return array.reshape(SHARD, GROUPS, -1, DH).transpose(1, 2, 0, 3)


def from_groups(array):
    return array.transpose(2, 0, 1, 3).reshape(SHARD, -1)


def split_three(array):
    high = lax.reduce_precision(array, 8, 7)
    rest = array - high
    middle = lax.reduce_precision(rest, 8, 7)
    low = rest - middle
    return jnp.stack([high.astype(BF), middle.astype(BF), low.astype(BF)], axis=1)


def shards(queries, key_states, value_states, outputs, out_grad, log_sums, selected):
    x, y, c = lax.axis_index("x"), lax.axis_index("y"), lax.axis_index("c")
    meta = jnp.stack([x, y, c]).astype(jnp.int32)

    kv_send = jnp.concatenate([by_group(key_states), by_group(value_states)], axis=1)

    lse = log_sums.reshape(4, 2, SHARD, HQG).transpose(0, 1, 3, 2).reshape(4, ROWS)
    chosen = jnp.broadcast_to(selected.reshape(1, TOPK).astype(F32), (4, TOPK))
    small = jnp.concatenate([lse, jnp.pad(chosen, ((0, 0), (0, 128 - TOPK)))], axis=1)
    kv_send, small = tie(kv_send, small)
    chunk = lambda d: lax.dynamic_index_in_dim(small, lax.rem(x + d, 4), 0, keepdims=False)
    move = lambda d: lax.ppermute(chunk(d), "x", [(i, (i + d) % 4) for i in range(4)])
    pieces = [chunk(0), move(3), move(2), move(1)]
    small = lax.dynamic_slice(jnp.stack(pieces + pieces), (lax.rem(4 - x, 4), 0), (4, ROWS + 128))
    lse_rows = split_three(small[:, :ROWS]).reshape(4, 12, DH)
    chosen_rows = small[:, ROWS:].astype(BF).reshape(4, 1, DH)
    small_rows = jnp.concatenate([lse_rows, chosen_rows], axis=1).reshape(4, 1, 13, DH)
    same = jnp.arange(2).reshape(1, 2, 1, 1) == lax.axis_index("h")
    small_rows = jnp.where(same, small_rows, 0).reshape(GROUPS, 13, DH)

    kv_own = lax.all_to_all(kv_send, ZH, split_axis=0, concat_axis=0, tiled=True)

    delta = jnp.sum(
        (out_grad.astype(F32) * outputs.astype(F32)).reshape(SHARD, GROUPS * HQG, DH), axis=-1
    )
    delta = delta.T.reshape(GROUPS, HQG * SHARD)
    delta_rows = split_three(delta).reshape(GROUPS, 6, DH)
    extra = [delta_rows, small_rows, jnp.zeros((GROUPS, EXTRA - 19, DH), BF)]
    (extra,) = tie(jnp.concatenate(extra, axis=1))
    qdo_send = jnp.concatenate(
        [by_group(queries).reshape(GROUPS, 256, DH), by_group(out_grad).reshape(GROUPS, 256, DH), extra],
        axis=1,
    )
    own = kv_own.reshape(1, 4, 2, 2, SHARD, DH)
    first = round_the_ring(own, 0)
    qdo_send = after(qdo_send, *first)
    qdo = lax.all_to_all(qdo_send, ZH, split_axis=0, concat_axis=0, tiled=True)
    row = jnp.concatenate([own] + first, axis=0)
    rows = [row] + round_the_ring(row, 1)

    qdo = after(qdo, *rows[1:])
    qdo_other = swap(qdo)
    extra = jnp.stack([qdo[:, ROWS:], qdo_other[:, ROWS:]]).reshape(8, 2, EXTRA, DH).astype(F32)
    delta = jnp.sum(extra[:, :, :6].reshape(8, 2, 3, 256), axis=2).reshape(8, 1, ROWS)
    extra = lax.dynamic_index_in_dim(extra, lax.axis_index("h"), 1, keepdims=False)
    lse = jnp.sum(extra[:, 6:18].reshape(8, 3, ROWS), axis=1).reshape(8, 1, ROWS)
    chosen = extra[:, 18, :TOPK].astype(jnp.int32)

    own, plus, minus, far, dq_own, dq_other = attend(meta, chosen, lse, delta, qdo, qdo_other, rows)
    dq = (dq_own + swap(dq_other)).astype(BF)
    query_grad = lax.all_to_all(dq, ZH, split_axis=0, concat_axis=0, tiled=True)
    part = sum([shift(a, 0, d).astype(F32) for a, d in ((far, 2), (plus, 1), (minus, -1))], own)
    part = after(part, query_grad)
    got = [shift(part[i].astype(BF), 1, d).astype(F32) for i, d in ((3, 2), (1, 1), (2, -1))]
    kv_grad = sum(got, part[0]).astype(BF).reshape(GROUPS, 2, SHARD, DH)
    kv_grad = lax.all_to_all(kv_grad, ZH, split_axis=0, concat_axis=0, tiled=True)
    return (
        from_groups(query_grad.reshape(GROUPS, HQG, SHARD, DH)),
        from_groups(kv_grad[:, :1]),
        from_groups(kv_grad[:, 1:]),
    )


def solution(mesh):
    wide = Mesh(mesh.devices.reshape(4, 4, 2, 4, 2), ("y", "z", "c", "x", "h"))
    rows = P(("y", "z", "c", "x", "h"), None)
    return jax.shard_map(
        shards,
        mesh=wide,
        in_specs=(
            rows,
            rows,
            rows,
            rows,
            rows,
            P(("y", "z", "c"), ("x", "h")),
            P(("y", "z", "c"), ("x", "h"), None),
        ),
        out_specs=(rows, rows, rows),
        check_vma=False,
    )
```

time: 207 us -> 171 us (0.83)
  waiting for transfers between devices: 97.1 us -> 57.9 us
  other arithmetic: 7.44 us -> 11.2 us
    ppermute x4 -> x3, waiting for transfers between devices: 14 us -> 0.01 us  [shards(): lax.ppermute(chunk(d), 'x', [(i, (i + d) % 4) for i in range(4)])]
    all_to_all x2, waiting for transfers between devices: 21 us -> 8.16 us  [the longest x1 6.63 us: shards(): lax.all_to_all(kv_grad, ZH, split_axis=0, concat_axis=0, tiled=True)]
    ppermute x14 -> x12, waiting for transfers between devices: 54.4 us -> 47.7 us  [shift(): return lax.ppermute(array, PLANE, pairs)]
    ppermute x14 -> x12, starting transfers between devices: 36.6 us -> 31.7 us  [shift(): return lax.ppermute(array, PLANE, pairs)]
    ppermute x6 -> x2, waiting for transfers between devices: 6.87 us -> 2.08 us  [swap(): return lax.ppermute(array, 'c', [(0, 1), (1, 0)])]
    all_to_all x1, starting transfers between devices: 3.49 us -> 7.21 us  [shards(): query_grad = lax.all_to_all(dq, ZH, split_axis=0, concat_axis=0, tiled=True)]
    ppermute x4 -> x3, starting transfers between devices: 8.25 us -> 4.83 us  [shards(): lax.ppermute(chunk(d), 'x', [(i, (i + d) % 4) for i in range(4)])]
    add x0 -> x1, other arithmetic: none -> 3.18 us  [shards(): sum([shift(a, 0, d).astype(F32) for a, d in ((far, 2), (plus, 1), (minus,...]
  transfers between devices with their start and end apart: 28 -> 21, of which waited for: 20 -> 12; matrix products, arithmetic and copies ran while one was open for 5% -> 7% of each run, Pallas kernels for 0% -> 0%
where the time goes in v2:
time: 171 us; the launch traced here: 169 us
  starting transfers between devices  65.5 us (38%)
  waiting for transfers between devices  57.9 us (34%)
  Pallas kernels  22.4 us (13%)
  other arithmetic  11.2 us (7%)
  local copies, waits for them, and re-layouts  10.6 us (6%)
    ppermute x12, waiting for transfers between devices, shift(): return lax.ppermute(array, PLANE, pairs)  47.7 us
    ppermute x12, starting transfers between devices, shift(): return lax.ppermute(array, PLANE, pairs)  31.7 us
    pallas_call x1, Pallas kernels, attend(): pl.pallas_call(kernel, out_shape=(shape(chunk, F32),) + (shape(chunk, BF)...  22.4 us
    all_to_all x1, starting transfers between devices, shards(): lax.all_to_all(kv_send, ZH, split_axis=0, concat_axis=0, tiled=True)  8.47 us
    all_to_all x1, starting transfers between devices, shards(): lax.all_to_all(kv_grad, ZH, split_axis=0, concat_axis=0, tiled=True)  7.21 us
    all_to_all x1, starting transfers between devices, shards(): query_grad = lax.all_to_all(dq, ZH, split_axis=0, concat_axis=0, tiled=True)  7.21 us
    all_to_all x1, waiting for transfers between devices, shards(): lax.all_to_all(kv_grad, ZH, split_axis=0, concat_axis=0, tiled=True)  6.63 us
    all_to_all x1, starting transfers between devices, shards(): qdo = lax.all_to_all(qdo_send, ZH, split_axis=0, concat_axis=0, tiled=True)  5.7 us
  transfers between devices with their start and end apart: 21, of which 12 were waited for; matrix products, arithmetic and copies ran while one was open for 7% of the time, Pallas kernels for 0%

profile of v2, /device:TPU:2, one launch (start us, length us, event | category | flops | bytes accessed | tf_op | source)
XLA Modules:
  0.0 168.7 jit_solution(15900872819684838481)
XLA Ops:
  4.9 8.5 %all-to-all-start = ((bf16[8,2,64,128]{3,2,1,0:T(8,128)(2,1)}), bf16[8,2,64,128]{3,2,1,0:T(8,128)(2,1)S(1)}, u32[]{:S(2)}, u32[]{:S(2)}) async-start(bf16[8,2,64,128]{3,2,1,0:T(8,128)(2,1)} %pad_maximum_fusion.2), calls=%async_computation | async-start | bytes 524288 | tf_op jit(solution)/shard_map/all_to_all | solution.py:221
  16.1 2.2 %collective-permute-start = (f32[640]{0:T(1024)S(1)}, f32[640]{0:T(1024)S(1)}, u32[]{:S(2)}, u32[]{:S(2)}) collective-permute-start(f32[640]{0:T(1024)S(1)} %get-tuple-element.27), channel_id=1, source_target_pairs={{0,6},{2,0},{4,2},{6,4},{1,7},{3,1},{5,3},{7,5},{8,14},{10,8},{12,... | collective-permute-start | bytes 7688 | tf_op jit(solution)/shard_map/ppermute | solution.py:212
  22.2 2.1 %collective-permute-start.5 = (bf16[1,4,2,2,64,128]{5,4,3,2,1,0:T(8,128)(2,1)S(1)}, bf16[1,4,2,2,64,128]{5,4,3,2,1,0:T(8,128)(2,1)S(1)}, u32[]{:S(2)}, u32[]{:S(2)}) collective-permute-start(bf16[1,4,2,2,64,128]{5,4,3,2,1,0:T(8,128)(2,1)S(1)} %bitcast.92), channel_id=1, source_target_pairs={{0,4},{2,6},{4,0},{6,2},{8,136},{10,138},{12,140},{14,142},{64,68}... | collective-permute-start | bytes 786440 | tf_op jit(solution)/shard_map/ppermute | solution.py:42
  27.6 2.6 %collective-permute-done.5 = bf16[1,4,2,2,64,128]{5,4,3,2,1,0:T(8,128)(2,1)S(1)} collective-permute-done((bf16[1,4,2,2,64,128]{5,4,3,2,1,0:T(8,128)(2,1)S(1)}, bf16[1,4,2,2,64,128]{5,4,3,2,1,0:T(8,128)(2,1)S(1)}, u32[]{:S(2)}, u32[]{:S(2)}) %collective-permute-start.5) | collective-permute-done | bytes 262176 | tf_op jit(solution)/shard_map/ppermute | solution.py:42
  30.2 2.8 %collective-permute-done.4 = bf16[1,4,2,2,64,128]{5,4,3,2,1,0:T(8,128)(2,1)S(1)} collective-permute-done((bf16[1,4,2,2,64,128]{5,4,3,2,1,0:T(8,128)(2,1)S(1)}, bf16[1,4,2,2,64,128]{5,4,3,2,1,0:T(8,128)(2,1)S(1)}, u32[]{:S(2)}, u32[]{:S(2)}) %collective-permute-start.4) | collective-permute-done | bytes 262176 | tf_op jit(solution)/shard_map/ppermute | solution.py:42
  33.0 5.7 %all-to-all-start.1 = ((bf16[8,544,128]{2,1,0:T(8,128)(2,1)}), bf16[8,544,128]{2,1,0:T(8,128)(2,1)S(1)}, u32[]{:S(2)}, u32[]{:S(2)}) async-start(bf16[8,544,128]{2,1,0:T(8,128)(2,1)} %pad_maximum_fusion), calls=%async_computation.1 | async-start | bytes 2228224 | tf_op jit(solution)/shard_map/all_to_all | solution.py:237
  38.9 3.3 %collective-permute-start.8 = (bf16[4,4,2,2,64,128]{5,4,3,2,1,0:T(8,128)(2,1)S(1)}, bf16[4,4,2,2,64,128]{5,4,3,2,1,0:T(8,128)(2,1)S(1)}, u32[]{:S(2)}, u32[]{:S(2)}) collective-permute-start(bf16[4,4,2,2,64,128]{5,4,3,2,1,0:T(8,128)(2,1)S(1)} %pad_maximum_fusion.1.w0), channel_id=1, source_target_pairs={{0,128},{2,130},{4,132},{6,134},{8,12},{10,14},{12,8},{14,10},{64,... | collective-permute-start | bytes 3145736 | tf_op jit(solution)/shard_map/ppermute | solution.py:42
  42.8 2.6 %collective-permute-start.6 = (bf16[4,4,2,2,64,128]{5,4,3,2,1,0:T(8,128)(2,1)S(1)}, bf16[4,4,2,2,64,128]{5,4,3,2,1,0:T(8,128)(2,1)}, u32[]{:S(2)}, u32[]{:S(2)}) collective-permute-start(bf16[4,4,2,2,64,128]{5,4,3,2,1,0:T(8,128)(2,1)S(1)} %pad_maximum_fusion.1.w0), channel_id=1, source_target_pairs={{0,192},{2,194},{4,196},{6,198},{8,14},{10,8},{12,10},{14,12},{64,... | collective-permute-start | bytes 3145736 | tf_op jit(solution)/shard_map/ppermute | solution.py:42
  45.4 10.0 %collective-permute-done.8.w3 = bf16[4,4,2,2,64,128]{5,4,3,2,1,0:T(8,128)(2,1)S(1)} collective-permute-done((bf16[4,4,2,2,64,128]{5,4,3,2,1,0:T(8,128)(2,1)S(1)}, bf16[4,4,2,2,64,128]{5,4,3,2,1,0:T(8,128)(2,1)S(1)}, u32[]{:S(2)}, u32[]{:S(2)}) %collective-permute-start.8) | collective-permute-done | bytes 1048608 | tf_op jit(solution)/shard_map/ppermute | solution.py:42
  55.4 11.1 %collective-permute-done.7.w2 = bf16[4,4,2,2,64,128]{5,4,3,2,1,0:T(8,128)(2,1)S(1)} collective-permute-done((bf16[4,4,2,2,64,128]{5,4,3,2,1,0:T(8,128)(2,1)S(1)}, bf16[4,4,2,2,64,128]{5,4,3,2,1,0:T(8,128)(2,1)S(1)}, u32[]{:S(2)}, u32[]{:S(2)}) %collective-permute-start.7) | collective-permute-done | bytes 1048608 | tf_op jit(solution)/shard_map/ppermute | solution.py:42
  68.5 2.1 %collective-permute-done.9.qdo_other = bf16[8,544,128]{2,1,0:T(8,128)(2,1)S(1)} collective-permute-done((bf16[8,544,128]{2,1,0:T(8,128)(2,1)S(1)}, bf16[8,544,128]{2,1,0:T(8,128)(2,1)S(1)}, u32[]{:S(2)}, u32[]{:S(2)}) %collective-permute-start.9) | collective-permute-done | bytes 1114144 | tf_op jit(solution)/shard_map/ppermute | solution.py:46
  73.0 22.4 %attend.1 = (f32[4,4,2,2,64,128]{5,4,3,2,1,0:T(8,128)}, bf16[4,4,2,2,64,128]{5,4,3,2,1,0:T(8,128)(2,1)}, bf16[4,4,2,2,64,128]{5,4,3,2,1,0:T(8,128)(2,1)}, bf16[4...) custom-call(s32[3]{0:T(128)} %pad_add_fusion.meta, s32[8,8]{1,0:T(8,128)} %fusion.7.chosen, ...), custom_call_target="tpu_custom_call" | custom-call | flops 20000000000 | bytes 20971520 | tf_op jit(solution)/shard_map/attend/pallas_call | solution.py:166
  95.5 2.9 %collective-permute-start.11 = (bf16[4,4,2,2,64,128]{5,4,3,2,1,0:T(8,128)(2,1)}, bf16[4,4,2,2,64,128]{5,4,3,2,1,0:T(8,128)(2,1)S(1)}, u32[]{:S(2)}, u32[]{:S(2)}) collective-permute-start(bf16[4,4,2,2,64,128]{5,4,3,2,1,0:T(8,128)(2,1)} %get-tuple-element.21), channel_id=1, source_target_pairs={{0,4},{2,6},{4,0},{6,2},{8,136},{10,138},{12,140},{14,142},{64,68}... | collective-permute-start | bytes 3145736 | tf_op jit(solution)/shard_map/ppermute | solution.py:42
  100.5 2.1 %add_convert_fusion = bf16[8,256,128]{2,1,0:T(8,128)(2,1)} fusion(f32[8,256,128]{2,1,0:T(8,128)} %get-tuple-element.18, f32[8,256,128]{2,1,0:T(8,128)S(1)} %collective-permute-done.10), kind=kLoop, calls=%fused_computation.3 | loop fusion | flops 524288 | bytes 2621440 | tf_op jit(solution)/shard_map/convert_element_type | solution.py:250
  102.6 7.2 %all-to-all-start.2 = ((bf16[8,256,128]{2,1,0:T(8,128)(2,1)}), bf16[8,256,128]{2,1,0:T(8,128)(2,1)S(1)}, u32[]{:S(2)}, u32[]{:S(2)}) async-start(bf16[8,256,128]{2,1,0:T(8,128)(2,1)} %add_convert_fusion), calls=%async_computation.2 | async-start | bytes 1048576 | tf_op jit(solution)/shard_map/all_to_all | solution.py:251
  109.8 2.4 %collective-permute-done.11 = bf16[4,4,2,2,64,128]{5,4,3,2,1,0:T(8,128)(2,1)S(1)} collective-permute-done((bf16[4,4,2,2,64,128]{5,4,3,2,1,0:T(8,128)(2,1)}, bf16[4,4,2,2,64,128]{5,4,3,2,1,0:T(8,128)(2,1)S(1)}, u32[]{:S(2)}, u32[]{:S(2)}) %collective-permute-start.11) | collective-permute-done | bytes 1048608 | tf_op jit(solution)/shard_map/ppermute | solution.py:42
  112.2 10.5 %collective-permute-done.12 = bf16[4,4,2,2,64,128]{5,4,3,2,1,0:T(8,128)(2,1)S(1)} collective-permute-done((bf16[4,4,2,2,64,128]{5,4,3,2,1,0:T(8,128)(2,1)}, bf16[4,4,2,2,64,128]{5,4,3,2,1,0:T(8,128)(2,1)S(1)}, u32[]{:S(2)}, u32[]{:S(2)}) %collective-permute-start.12) | collective-permute-done | bytes 1048608 | tf_op jit(solution)/shard_map/ppermute | solution.py:42
  123.7 3.2 %convert_add_fusion = f32[4,4,2,2,64,128]{5,4,3,2,1,0:T(8,128)S(1)} fusion(bf16[4,4,2,2,64,128]{5,4,3,2,1,0:T(8,128)(2,1)} %collective-permute-done.13, bf16[4,4,2,2,64,128]{5,4,3,2,1,0:T(8,128)(2,1)} %copy-done.3, f32[4,4,2,2,64,128]{5,4,3,2,1,0:T(8,128)} %get-tuple-element.20, bf16[4,4,2,2,64,128]{5,4,3,2,1,0:T(8,128)(2,1)} %copy-done.2), kind=kLoop, calls=%fused_computation | loop fusion | flops 3145728 | bytes 7340032 | tf_op jit(solution)/shard_map/add | solution.py:252
  127.2 11.2 %collective-permute-start.14 = (bf16[4,2,2,64,128]{4,3,2,1,0:T(8,128)(2,1)S(1)}, bf16[4,2,2,64,128]{4,3,2,1,0:T(8,128)(2,1)S(1)}, u32[]{:S(2)}, u32[]{:S(2)}) collective-permute-start(bf16[4,2,2,64,128]{4,3,2,1,0:T(8,128)(2,1)S(1)} %get-tuple-element.28), channel_id=1, source_target_pairs={{0,128},{2,130},{4,132},{6,134},{8,12},{10,14},{12,8},{14,10},{64,... | collective-permute-start | bytes 786440 | tf_op jit(solution)/shard_map/ppermute | solution.py:42
  138.4 4.9 %collective-permute-start.16 = (bf16[4,2,2,64,128]{4,3,2,1,0:T(8,128)(2,1)S(1)}, bf16[4,2,2,64,128]{4,3,2,1,0:T(8,128)(2,1)S(1)}, u32[]{:S(2)}, u32[]{:S(2)}) collective-permute-start(bf16[4,2,2,64,128]{4,3,2,1,0:T(8,128)(2,1)S(1)} %get-tuple-element.29), channel_id=1, source_target_pairs={{0,192},{2,194},{4,196},{6,198},{8,14},{10,8},{12,10},{14,12},{64,... | collective-permute-start | bytes 786440 | tf_op jit(solution)/shard_map/ppermute | solution.py:42
  143.3 4.5 %collective-permute-done.16 = bf16[4,2,2,64,128]{4,3,2,1,0:T(8,128)(2,1)S(1)} collective-permute-done((bf16[4,2,2,64,128]{4,3,2,1,0:T(8,128)(2,1)S(1)}, bf16[4,2,2,64,128]{4,3,2,1,0:T(8,128)(2,1)S(1)}, u32[]{:S(2)}, u32[]{:S(2)}) %collective-permute-start.16) | collective-permute-done | bytes 262176 | tf_op jit(solution)/shard_map/ppermute | solution.py:42
  147.8 3.1 %collective-permute-done.15 = bf16[4,2,2,64,128]{4,3,2,1,0:T(8,128)(2,1)S(1)} collective-permute-done((bf16[4,2,2,64,128]{4,3,2,1,0:T(8,128)(2,1)S(1)}, bf16[4,2,2,64,128]{4,3,2,1,0:T(8,128)(2,1)S(1)}, u32[]{:S(2)}, u32[]{:S(2)}) %collective-permute-start.15) | collective-permute-done | bytes 262176 | tf_op jit(solution)/shard_map/ppermute | solution.py:42
  151.7 7.2 %all-to-all-start.3 = ((bf16[8,2,64,128]{3,2,1,0:T(8,128)(2,1)}), bf16[8,2,64,128]{3,2,1,0:T(8,128)(2,1)S(1)}, u32[]{:S(2)}, u32[]{:S(2)}) async-start(bf16[8,2,64,128]{3,2,1,0:T(8,128)(2,1)} %bitcast.30), calls=%async_computation.3 | async-start | bytes 524288 | tf_op jit(solution)/shard_map/all_to_all | solution.py:256
  160.5 6.6 %all-to-all-done.3 = bf16[8,2,64,128]{3,2,1,0:T(8,128)(2,1)S(1)} async-done(((bf16[8,2,64,128]{3,2,1,0:T(8,128)(2,1)}), bf16[8,2,64,128]{3,2,1,0:T(8,128)(2,1)S(1)}, u32[]{:S(2)}, u32[]{:S(2)}) %all-to-all-start.3) | async-done | bytes 262176 | tf_op jit(solution)/shard_map/all_to_all | solution.py:256
  (111 shorter events, 26.6 us)
Async XLA Ops:
  0.6 17.6 %copy-start = (bf16[64,4096]{1,0:T(8,128)(2,1)S(1)}, bf16[64,4096]{1,0:T(8,128)(2,1)}, u32[]{:S(2)}) copy-start(bf16[64,4096]{1,0:T(8,128)(2,1)} %param.11) | copy-start | bytes 1572868
  0.6 17.6 %copy-start.6 = (bf16[64,4096]{1,0:T(8,128)(2,1)S(1)}, bf16[64,4096]{1,0:T(8,128)(2,1)}, u32[]{:S(2)}) copy-start(bf16[64,4096]{1,0:T(8,128)(2,1)} %param.10) | copy-start | bytes 1572868
  4.9 17.3 %all-to-all-start = ((bf16[8,2,64,128]{3,2,1,0:T(8,128)(2,1)}), bf16[8,2,64,128]{3,2,1,0:T(8,128)(2,1)S(1)}, u32[]{:S(2)}, u32[]{:S(2)}) async-start(bf16[8,2,64,128]{3,2,1,0:T(8,128)(2,1)} %pad_maximum_fusion.2), calls=%async_computation | async-start | bytes 524288 | tf_op jit(solution)/shard_map/all_to_all | solution.py:221
  13.4 7.0 %collective-permute-start.2 = (f32[640]{0:T(1024)S(1)}, f32[640]{0:T(1024)S(1)}, u32[]{:S(2)}, u32[]{:S(2)}) collective-permute-start(f32[640]{0:T(1024)S(1)} %get-tuple-element.25), channel_id=1, source_target_pairs={{0,2},{2,4},{4,6},{6,0},{1,3},{3,5},{5,7},{7,1},{8,10},{10,12},{12... | collective-permute-start | bytes 7688 | tf_op jit(solution)/shard_map/ppermute | solution.py:212
  15.0 5.5 %collective-permute-start.1 = (f32[640]{0:T(1024)S(1)}, f32[640]{0:T(1024)S(1)}, u32[]{:S(2)}, u32[]{:S(2)}) collective-permute-start(f32[640]{0:T(1024)S(1)} %get-tuple-element.26), channel_id=1, source_target_pairs={{0,4},{2,6},{4,0},{6,2},{1,5},{3,7},{5,1},{7,3},{8,12},{10,14},{12... | collective-permute-start | bytes 7688 | tf_op jit(solution)/shard_map/ppermute | solution.py:212
  16.1 4.4 %collective-permute-start = (f32[640]{0:T(1024)S(1)}, f32[640]{0:T(1024)S(1)}, u32[]{:S(2)}, u32[]{:S(2)}) collective-permute-start(f32[640]{0:T(1024)S(1)} %get-tuple-element.27), channel_id=1, source_target_pairs={{0,6},{2,0},{4,2},{6,4},{1,7},{3,1},{5,3},{7,5},{8,14},{10,8},{12,... | collective-permute-start | bytes 7688 | tf_op jit(solution)/shard_map/ppermute | solution.py:212
  22.2 8.0 %collective-permute-start.5 = (bf16[1,4,2,2,64,128]{5,4,3,2,1,0:T(8,128)(2,1)S(1)}, bf16[1,4,2,2,64,128]{5,4,3,2,1,0:T(8,128)(2,1)S(1)}, u32[]{:S(2)}, u32[]{:S(2)}) collective-permute-start(bf16[1,4,2,2,64,128]{5,4,3,2,1,0:T(8,128)(2,1)S(1)} %bitcast.92), channel_id=1, source_target_pairs={{0,4},{2,6},{4,0},{6,2},{8,136},{10,138},{12,140},{14,142},{64,68}... | collective-permute-start | bytes 786440 | tf_op jit(solution)/shard_map/ppermute | solution.py:42
  24.4 8.6 %collective-permute-start.4 = (bf16[1,4,2,2,64,128]{5,4,3,2,1,0:T(8,128)(2,1)S(1)}, bf16[1,4,2,2,64,128]{5,4,3,2,1,0:T(8,128)(2,1)S(1)}, u32[]{:S(2)}, u32[]{:S(2)}) collective-permute-start(bf16[1,4,2,2,64,128]{5,4,3,2,1,0:T(8,128)(2,1)S(1)} %bitcast.93), channel_id=1, source_target_pairs={{0,2},{2,4},{4,6},{6,0},{8,72},{10,74},{12,76},{14,78},{64,66},{66... | collective-permute-start | bytes 786440 | tf_op jit(solution)/shard_map/ppermute | solution.py:42
  24.4 8.6 %collective-permute-start.3 = (bf16[1,4,2,2,64,128]{5,4,3,2,1,0:T(8,128)(2,1)S(1)}, bf16[1,4,2,2,64,128]{5,4,3,2,1,0:T(8,128)(2,1)S(1)}, u32[]{:S(2)}, u32[]{:S(2)}) collective-permute-start(bf16[1,4,2,2,64,128]{5,4,3,2,1,0:T(8,128)(2,1)S(1)} %bitcast.94), channel_id=1, source_target_pairs={{0,6},{2,0},{4,2},{6,4},{8,200},{10,202},{12,204},{14,206},{64,70}... | collective-permute-start | bytes 786440 | tf_op jit(solution)/shard_map/ppermute | solution.py:42
  33.0 34.5 %all-to-all-start.1 = ((bf16[8,544,128]{2,1,0:T(8,128)(2,1)}), bf16[8,544,128]{2,1,0:T(8,128)(2,1)S(1)}, u32[]{:S(2)}, u32[]{:S(2)}) async-start(bf16[8,544,128]{2,1,0:T(8,128)(2,1)} %pad_maximum_fusion), calls=%async_computation.1 | async-start | bytes 2228224 | tf_op jit(solution)/shard_map/all_to_all | solution.py:237
  38.8 34.1 %copy-start.4 = (bf16[4,4,2,2,64,128]{5,4,3,2,1,0:T(8,128)(2,1)}, bf16[4,4,2,2,64,128]{5,4,3,2,1,0:T(8,128)(2,1)S(1)}, u32[]{:S(2)}) copy-start(bf16[4,4,2,2,64,128]{5,4,3,2,1,0:T(8,128)(2,1)S(1)} %pad_maximum_fusion.1.w0) | copy-start | bytes 3145732
  38.9 16.5 %collective-permute-start.8 = (bf16[4,4,2,2,64,128]{5,4,3,2,1,0:T(8,128)(2,1)S(1)}, bf16[4,4,2,2,64,128]{5,4,3,2,1,0:T(8,128)(2,1)S(1)}, u32[]{:S(2)}, u32[]{:S(2)}) collective-permute-start(bf16[4,4,2,2,64,128]{5,4,3,2,1,0:T(8,128)(2,1)S(1)} %pad_maximum_fusion.1.w0), channel_id=1, source_target_pairs={{0,128},{2,130},{4,132},{6,134},{8,12},{10,14},{12,8},{14,10},{64,... | collective-permute-start | bytes 3145736 | tf_op jit(solution)/shard_map/ppermute | solution.py:42
  42.1 24.3 %collective-permute-start.7 = (bf16[4,4,2,2,64,128]{5,4,3,2,1,0:T(8,128)(2,1)S(1)}, bf16[4,4,2,2,64,128]{5,4,3,2,1,0:T(8,128)(2,1)S(1)}, u32[]{:S(2)}, u32[]{:S(2)}) collective-permute-start(bf16[4,4,2,2,64,128]{5,4,3,2,1,0:T(8,128)(2,1)S(1)} %pad_maximum_fusion.1.w0), channel_id=1, source_target_pairs={{0,64},{2,66},{4,68},{6,70},{8,10},{10,12},{12,14},{14,8},{64,128}... | collective-permute-start | bytes 3145736 | tf_op jit(solution)/shard_map/ppermute | solution.py:42
  42.8 24.7 %collective-permute-start.6 = (bf16[4,4,2,2,64,128]{5,4,3,2,1,0:T(8,128)(2,1)S(1)}, bf16[4,4,2,2,64,128]{5,4,3,2,1,0:T(8,128)(2,1)}, u32[]{:S(2)}, u32[]{:S(2)}) collective-permute-start(bf16[4,4,2,2,64,128]{5,4,3,2,1,0:T(8,128)(2,1)S(1)} %pad_maximum_fusion.1.w0), channel_id=1, source_target_pairs={{0,192},{2,194},{4,196},{6,198},{8,14},{10,8},{12,10},{14,12},{64,... | collective-permute-start | bytes 3145736 | tf_op jit(solution)/shard_map/ppermute | solution.py:42
  67.6 3.0 %collective-permute-start.9 = (bf16[8,544,128]{2,1,0:T(8,128)(2,1)S(1)}, bf16[8,544,128]{2,1,0:T(8,128)(2,1)S(1)}, u32[]{:S(2)}, u32[]{:S(2)}) collective-permute-start(bf16[8,544,128]{2,1,0:T(8,128)(2,1)S(1)} %all-to-all-done.1.qdo_own), channel_id=1, source_target_pairs={{0,8},{8,0},{1,9},{9,1},{2,10},{10,2},{3,11},{11,3},{4,12},{12,4},... | collective-permute-start | bytes 3342344 | tf_op jit(solution)/shard_map/ppermute | solution.py:46
  95.4 5.1 %collective-permute-start.10 = (f32[8,256,128]{2,1,0:T(8,128)}, f32[8,256,128]{2,1,0:T(8,128)S(1)}, u32[]{:S(2)}, u32[]{:S(2)}) collective-permute-start(f32[8,256,128]{2,1,0:T(8,128)} %get-tuple-element.19), channel_id=1, source_target_pairs={{0,8},{8,0},{1,9},{9,1},{2,10},{10,2},{3,11},{11,3},{4,12},{12,4},... | collective-permute-start | bytes 3145736 | tf_op jit(solution)/shard_map/ppermute | solution.py:46
  95.5 16.7 %collective-permute-start.11 = (bf16[4,4,2,2,64,128]{5,4,3,2,1,0:T(8,128)(2,1)}, bf16[4,4,2,2,64,128]{5,4,3,2,1,0:T(8,128)(2,1)S(1)}, u32[]{:S(2)}, u32[]{:S(2)}) collective-permute-start(bf16[4,4,2,2,64,128]{5,4,3,2,1,0:T(8,128)(2,1)} %get-tuple-element.21), channel_id=1, source_target_pairs={{0,4},{2,6},{4,0},{6,2},{8,136},{10,138},{12,140},{14,142},{64,68}... | collective-permute-start | bytes 3145736 | tf_op jit(solution)/shard_map/ppermute | solution.py:42
  98.4 24.3 %collective-permute-start.12 = (bf16[4,4,2,2,64,128]{5,4,3,2,1,0:T(8,128)(2,1)}, bf16[4,4,2,2,64,128]{5,4,3,2,1,0:T(8,128)(2,1)S(1)}, u32[]{:S(2)}, u32[]{:S(2)}) collective-permute-start(bf16[4,4,2,2,64,128]{5,4,3,2,1,0:T(8,128)(2,1)} %get-tuple-element.22), channel_id=1, source_target_pairs={{0,2},{2,4},{4,6},{6,0},{8,72},{10,74},{12,76},{14,78},{64,66},{66... | collective-permute-start | bytes 3145736 | tf_op jit(solution)/shard_map/ppermute | solution.py:42
  98.5 25.0 %collective-permute-start.13 = (bf16[4,4,2,2,64,128]{5,4,3,2,1,0:T(8,128)(2,1)}, bf16[4,4,2,2,64,128]{5,4,3,2,1,0:T(8,128)(2,1)}, u32[]{:S(2)}, u32[]{:S(2)}) collective-permute-start(bf16[4,4,2,2,64,128]{5,4,3,2,1,0:T(8,128)(2,1)} %get-tuple-element.23), channel_id=1, source_target_pairs={{0,6},{2,0},{4,2},{6,4},{8,200},{10,202},{12,204},{14,206},{64,70}... | collective-permute-start | bytes 3145736 | tf_op jit(solution)/shard_map/ppermute | solution.py:42
  102.6 24.3 %all-to-all-start.2 = ((bf16[8,256,128]{2,1,0:T(8,128)(2,1)}), bf16[8,256,128]{2,1,0:T(8,128)(2,1)S(1)}, u32[]{:S(2)}, u32[]{:S(2)}) async-start(bf16[8,256,128]{2,1,0:T(8,128)(2,1)} %add_convert_fusion), calls=%async_computation.2 | async-start | bytes 1048576 | tf_op jit(solution)/shard_map/all_to_all | solution.py:251
  127.2 16.1 %collective-permute-start.14 = (bf16[4,2,2,64,128]{4,3,2,1,0:T(8,128)(2,1)S(1)}, bf16[4,2,2,64,128]{4,3,2,1,0:T(8,128)(2,1)S(1)}, u32[]{:S(2)}, u32[]{:S(2)}) collective-permute-start(bf16[4,2,2,64,128]{4,3,2,1,0:T(8,128)(2,1)S(1)} %get-tuple-element.28), channel_id=1, source_target_pairs={{0,128},{2,130},{4,132},{6,134},{8,12},{10,14},{12,8},{14,10},{64,... | collective-permute-start | bytes 786440 | tf_op jit(solution)/shard_map/ppermute | solution.py:42
  138.4 9.4 %collective-permute-start.16 = (bf16[4,2,2,64,128]{4,3,2,1,0:T(8,128)(2,1)S(1)}, bf16[4,2,2,64,128]{4,3,2,1,0:T(8,128)(2,1)S(1)}, u32[]{:S(2)}, u32[]{:S(2)}) collective-permute-start(bf16[4,2,2,64,128]{4,3,2,1,0:T(8,128)(2,1)S(1)} %get-tuple-element.29), channel_id=1, source_target_pairs={{0,192},{2,194},{4,196},{6,198},{8,14},{10,8},{12,10},{14,12},{64,... | collective-permute-start | bytes 786440 | tf_op jit(solution)/shard_map/ppermute | solution.py:42
  143.3 7.6 %collective-permute-start.15 = (bf16[4,2,2,64,128]{4,3,2,1,0:T(8,128)(2,1)S(1)}, bf16[4,2,2,64,128]{4,3,2,1,0:T(8,128)(2,1)S(1)}, u32[]{:S(2)}, u32[]{:S(2)}) collective-permute-start(bf16[4,2,2,64,128]{4,3,2,1,0:T(8,128)(2,1)S(1)} %get-tuple-element.30), channel_id=1, source_target_pairs={{0,64},{2,66},{4,68},{6,70},{8,10},{10,12},{12,14},{14,8},{64,128}... | collective-permute-start | bytes 786440 | tf_op jit(solution)/shard_map/ppermute | solution.py:42
  151.7 15.4 %all-to-all-start.3 = ((bf16[8,2,64,128]{3,2,1,0:T(8,128)(2,1)}), bf16[8,2,64,128]{3,2,1,0:T(8,128)(2,1)S(1)}, u32[]{:S(2)}, u32[]{:S(2)}) async-start(bf16[8,2,64,128]{3,2,1,0:T(8,128)(2,1)} %bitcast.30), calls=%async_computation.3 | async-start | bytes 524288 | tf_op jit(solution)/shard_map/all_to_all | solution.py:256
  (7 other events, 33.5 us)
